TPU v7x, 128 devices: a whole 4x4x4 slice. The times are simulated.
128 devices in a mesh: bx: 8 (over x, core), by: 16 (over z, y).
Axes of the slice: x: 4, y: 4, z: 4, core: 2. Of those that a mesh axis runs over, the one named last changes fastest.
Arguments:
- features: bfloat16 [1024, 8, 8, 512], P(('bx', 'by')), may hold values from -6 to 6
- neighbour_ids: int32 [1024, 27], P(('bx', 'by')), may hold values from -1 to 1023, as said below
- conv_weight: bfloat16 [27, 64, 64], replicated, may hold values from -0.15625 to 0.15625
- conv_bias: float32 [64], replicated, may hold values from -3 to 3
- down_weight: bfloat16 [8, 64, 128], replicated, may hold values from -0.25 to 0.25
- coarse_owner: int32 [1024, 1], P(('bx', 'by')), may hold values from 0 to 15; in each aligned block of 8 rows (0 to 7, 8 to 15, ...) at most 2 rows name the same one
Outputs:
- coarse_bricks: bfloat16 [4096, 4, 4, 512], P(('bx', 'by'))
Inputs may be any that keep to these rules, and one draw needn't show every extreme that they name: `neighbour_ids`: entry 13 of each brick is the brick itself. Every other entry (sx+1)*9+(sy+1)*3+(sz+1) of a brick on device (i, j) is -1 or a brick on a device whose bx index is i or i+sx and whose by index is j or j+sy. `coarse_owner`: among the bricks of one device, at most 2 have the same owner.
All inputs are finite; a program needn't handle non-finite values.
Results may differ from a plain program's by a relative error of at most 0.0049.
Values may be sent and summed in bfloat16 or wider, within the bound.
A program may use at most 64 MiB of HBM per device.

v0:
```python
import jax
import jax.numpy as jnp
from jax import lax
from jax.sharding import PartitionSpec as P

offsets = (-1, 0, 1)


def extended(x, sides, width):
    for axis, dim in sides:
        size, length = (lax.axis_size(axis), x.shape[dim])
        up = [(i, (i + 1) % size) for i in range(size - 1)]
        down = [(j, i) for i, j in up]
        last = lax.slice_in_dim(x, length - width, length, axis=dim)
        first = lax.slice_in_dim(x, 0, width, axis=dim)
        before = lax.ppermute(last, axis, up)
        after = lax.ppermute(first, axis, down)
        x = jnp.concatenate([before, x, after], axis=dim)
    return x


def layer_slice(step):
    if step < 0:
        return slice(7, 8)
    if step == 0:
        return slice(0, 8)
    return slice(0, 1)


def depth_slice(step, chans):
    if step < 0:
        return slice(7 * chans, 8 * chans)
    if step == 0:
        return slice(0, 8 * chans)
    return slice(0, chans)


def banded_conv(conv_weight, tap_x, tap_y, chans):
    zeros = jnp.zeros((chans, chans), conv_weight.dtype)
    row_list = []
    for depth_in in range(10):
        blocks = []
        for depth_out in range(8):
            tap_z = depth_in - depth_out
            if 0 <= tap_z <= 2:
                blocks.append(conv_weight[tap_x * 9 + tap_y * 3 + tap_z])
            else:
                blocks.append(zeros)
        row_list.append(jnp.concatenate(blocks, 1))
    return jnp.concatenate(row_list, 0)


def banded_down(down_weight, chans, out_chans):
    zeros = jnp.zeros((chans, out_chans), down_weight.dtype)
    pairs = []
    for first in range(2):
        seconds = []
        for second in range(2):
            row_list = []
            for depth_in in range(8):
                blocks = []
                for depth_out in range(4):
                    if depth_in // 2 == depth_out:
                        blocks.append(down_weight[first * 4 + second * 2 + depth_in % 2])
                    else:
                        blocks.append(zeros)
                row_list.append(jnp.concatenate(blocks, 1))
            seconds.append(jnp.concatenate(row_list, 0))
        pairs.append(jnp.stack(seconds, 0))
    return jnp.stack(pairs, 0)


def shards(features, neighbour_ids, conv_weight, conv_bias, down_weight, coarse_owner):
    bricks = features.shape[0]
    chans = conv_weight.shape[1]
    out_chans = down_weight.shape[2]
    count_y = lax.axis_size("by")
    index_x = lax.axis_index("bx")
    index_y = lax.axis_index("by")
    source_dev = jnp.maximum(neighbour_ids, 0) // bricks
    delta_x = source_dev // count_y - index_x
    delta_y = source_dev % count_y - index_y
    local_brick = jnp.maximum(neighbour_ids, 0) % bricks
    present = neighbour_ids >= 0
    beside_all = extended(features[None, None], (("bx", 0), ("by", 1)), 1)
    beside_all = beside_all.reshape(9 * bricks, 8, 8, 8 * chans)
    local_ids = ((delta_x + 1) * 3 + (delta_y + 1)) * bricks + local_brick
    local_ids = jnp.where(present, local_ids, 0)
    plane_x = []
    for shift_x in offsets:
        plane_y = []
        for shift_y in offsets:
            plane_z = []
            for shift_z in offsets:
                if shift_x == 0 and shift_y == 0 and (shift_z == 0):
                    plane_z.append(features)
                    continue
                column = (shift_x + 1) * 9 + (shift_y + 1) * 3 + (shift_z + 1)
                taken = jnp.take(
                    beside_all[
                        :, layer_slice(shift_x), layer_slice(shift_y), depth_slice(shift_z, chans)
                    ],
                    local_ids[:, column],
                    axis=0,
                )
                taken = jnp.where(
                    present[:, column][:, None, None, None], taken, jnp.zeros((), taken.dtype)
                )
                plane_z.append(taken)
            plane_y.append(jnp.concatenate(plane_z, 3))
        plane_x.append(jnp.concatenate(plane_y, 2))
    padded = jnp.concatenate(plane_x, 1)
    total = jnp.zeros((bricks, 8, 8, 8 * chans), jnp.float32)
    for tap_x in range(3):
        for tap_y in range(3):
            window = padded[:, tap_x : tap_x + 8, tap_y : tap_y + 8]
            total = total + jnp.dot(
                window,
                banded_conv(conv_weight, tap_x, tap_y, chans),
                preferred_element_type=jnp.float32,
            )
    bias_row = jnp.tile(conv_bias, 8)
    hidden = (features.astype(jnp.float32) + jax.nn.silu(total + bias_row)).astype(jnp.bfloat16)
    split = hidden.reshape(bricks, 4, 2, 4, 2, 8 * chans)
    kernel = banded_down(down_weight, chans, out_chans)
    coarse = jnp.einsum(
        "nxaybk,abko->nxyo", split, kernel, preferred_element_type=jnp.float32
    ).astype(jnp.bfloat16)
    coarse_flat = coarse.reshape(bricks, 64 * out_chans)
    capacity = max(2, 12 * bricks // (5 * count_y))
    owners = coarse_owner[:, 0]
    onehot = (owners[:, None] == jnp.arange(count_y, dtype=jnp.int32)[None, :]).astype(jnp.float32)
    earlier = (jnp.arange(bricks)[:, None] > jnp.arange(bricks)[None, :]).astype(jnp.float32)
    ranks = jnp.sum(
        jnp.dot(earlier, onehot, precision=lax.Precision.HIGHEST) * onehot, axis=1
    ).astype(jnp.int32)
    slots = owners * capacity + ranks
    placing = (jnp.arange(count_y * capacity, dtype=jnp.int32)[:, None] == slots[None, :]).astype(
        jnp.bfloat16
    )
    outgoing = jnp.dot(placing, coarse_flat, preferred_element_type=jnp.float32).astype(
        jnp.bfloat16
    )
    outgoing = outgoing.reshape(count_y * capacity, 4, 4, 4 * out_chans)
    return lax.all_to_all(outgoing, "by", split_axis=0, concat_axis=0, tiled=True)


def solution(mesh):
    in_specs = (
        P(("bx", "by"), None, None, None),
        P(("bx", "by"), None),
        P(),
        P(),
        P(),
        P(("bx", "by"), None),
    )
    out_specs = P(("bx", "by"), None, None, None)
    return jax.shard_map(shards, mesh=mesh, in_specs=in_specs, out_specs=out_specs, check_vma=False)
```

profile of v0, /device:TPU:0, one launch (start us, length us, event | category | flops | bytes accessed | tf_op | source)
XLA Modules:
  0.0 224.3 jit_solution(16639200123712829371)
XLA Ops:
  0.0 1.3 collective-permute-start.1
  1.3 3.1 %collective-permute-start = (bf16[1,1,8,8,8,512]{5,4,3,2,1,0:T(8,128)(2,1)}, bf16[1,1,8,8,8,512]{5,4,3,2,1,0:T(8,128)(2,1)S(1)}, u32[]{:S(2)}, u32[]{:S(2)}) collective-permute-start(bf16[1,1,8,8,8,512]{5,4,3,2,1,0:T(8,128)(2,1)} %bitcast.244), channel_id=1, source_target_pairs={{0,16},{16,32},{32,48},{48,64},{64,80},{80,96},{96,112},{1,17},{17... | collective-permute-start | bytes 1572872 | tf_op jit(solution)/shard_map/ppermute | solution.py:16
  71.3 1.4 pad_maximum_fusion.1
  72.6 1.3 collective-permute-start.3
  73.9 5.7 %collective-permute-start.2 = (bf16[3,1,8,8,8,512]{5,4,3,2,1,0:T(8,128)(2,1)}, bf16[3,1,8,8,8,512]{5,4,3,2,1,0:T(8,128)(2,1)}, u32[]{:S(2)}, u32[]{:S(2)}) collective-permute-start(bf16[3,1,8,8,8,512]{5,4,3,2,1,0:T(8,128)(2,1)} %pad_maximum_fusion.1), channel_id=1, source_target_pairs={{0,1},{1,2},{2,3},{3,4},{4,5},{5,6},{6,7},{7,8},{8,9},{9,10},{10,1... | collective-permute-start | bytes 4718600 | tf_op jit(solution)/shard_map/ppermute | solution.py:16
  84.4 27.4 %collective-permute-done.3 = bf16[3,1,8,8,8,512]{5,4,3,2,1,0:T(8,128)(2,1)S(1)} collective-permute-done((bf16[3,1,8,8,8,512]{5,4,3,2,1,0:T(8,128)(2,1)}, bf16[3,1,8,8,8,512]{5,4,3,2,1,0:T(8,128)(2,1)S(1)}, u32[]{:S(2)}, u32[]{:S(2)}) %collective-permute-start.3) | collective-permute-done | bytes 1572896 | tf_op jit(solution)/shard_map/ppermute | solution.py:17
  111.8 1.7 collective-permute-done.2
  113.5 1.7 pad_maximum_fusion
  115.2 2.7 %copy.43 = bf16[3,3,8,8,8,512]{5,2,1,0,4,3:T(8,128)(2,1)S(1)} copy(bf16[3,3,8,8,8,512]{5,4,3,2,1,0:T(8,128)(2,1)S(1)} %pad_maximum_fusion) | data formatting | bytes 9437184 | tf_op jit(solution)/shard_map/concatenate | solution.py:18
  129.6 2.2 gather_fusion.16
  131.8 2.2 gather_fusion.14
  134.0 2.3 %gather_fusion.15 = bf16[8,8,512]{2,1,0:T(8,128)(2,1)} fusion(bf16[72,8,512]{2,1,0:T(8,128)(2,1)} %copy.63, s32[1024]{0:T(1024)} %pad_clamp_fusion.10), kind=kCustom, calls=%fused_computation.24.clone | custom fusion | bytes 131104 | tf_op jit(solution)/shard_map/jit(_take)/gather | solution.py:99
  136.3 2.4 %gather_fusion.10 = bf16[8,8,512]{2,1,0:T(8,128)(2,1)} fusion(bf16[72,8,512]{2,1,0:T(8,128)(2,1)} %copy.55, s32[1024]{0:T(1024)} %pad_clamp_fusion.15), kind=kCustom, calls=%fused_computation.5.clone | custom fusion | bytes 131104 | tf_op jit(solution)/shard_map/jit(_take)/gather | solution.py:99
  138.7 1.3 gather_fusion.13
  141.0 1.6 gather_fusion.11
  142.6 1.6 gather_fusion.9
  144.2 1.4 gather_fusion.17
  145.6 1.4 gather_fusion.8
  147.0 1.6 gather_fusion.7
  148.6 1.4 gather_fusion.6
  150.0 1.6 gather_fusion.5
  151.6 1.7 gather_fusion.4
  153.3 1.6 gather_fusion.3
  154.9 1.4 gather_fusion.2
  156.3 1.6 gather_fusion.1
  157.9 1.4 gather_fusion
  166.2 1.2 broadcast_select_fusion.2
  168.0 5.4 %maximum_maximum_fusion = bf16[8,9,10,640]{3,2,1,0:T(8,128)(2,1)S(1)} fusion(bf16[8,8,1,64]{3,2,1,0:T(2,128)(2,1)S(1)} %get-tuple-element.177, bf16[8,8,1,512]{3,2,1,0:T(2,128)(2,1)S(1)} %get-tuple-element.173, bf16[8,8,1,64]{3,2,1,0:T(2,128)(2,1)S(1)} %get-tuple-element.178, bf16[8,8,8,64]{3,2,1,0:T(8,128)(2,1)S(1)} %get-tuple-element.175, ...), kind=kLoop, calls=%fused_computation.33 | loop fusion | flops 16588800 | bytes 1843200 | tf_op jit(solution)/shard_map/concatenate | solution.py:112
  183.4 1.6 gather_fusion.22
  185.0 1.5 gather_fusion.20
  187.7 8.3 %maximum_maximum_fusion.1 = bf16[8,9,10,640]{3,2,1,0:T(8,128)(2,1)S(1)} fusion(bf16[8,1,1,64]{3,2,1,0:T(2,128)(2,1)S(1)} %broadcast_select_fusion.28, bf16[8,1,1,512]{3,2,1,0:T(2,128)(2,1)S(1)} %get-tuple-element.181, bf16[8,1,1,64]{3,2,1,0:T(2,128)(2,1)S(1)} %get-tuple-element.185, bf16[8,1,8,64]{3,2,1,0:T(8,128)(2,1)S(1)} %get-tuple-element.183, ...), kind=kLoop, calls=%fused_computation.34 | loop fusion | flops 16588800 | bytes 1843200 | tf_op jit(solution)/shard_map/concatenate | solution.py:112
  201.2 22.3 %all_to_all.5 = bf16[32,4,4,512]{3,2,1,0:T(4,128)(2,1)S(1)} all-to-all(bf16[32,4,4,512]{3,2,1,0:T(4,128)(2,1)S(1)} %reshape.217), channel_id=1, replica_groups=mesh['bx'=8,'by'=16] {'by'}, dimensions={0} | all-to-all | bytes 1048576 | tf_op jit(solution)/shard_map/all_to_all | solution.py:145
  (535 shorter events, 106.5 us)
Async XLA Ops:
  0.0 71.2 %collective-permute-start.1 = (bf16[1,1,8,8,8,512]{5,4,3,2,1,0:T(8,128)(2,1)}, bf16[1,1,8,8,8,512]{5,4,3,2,1,0:T(8,128)(2,1)S(1)}, u32[]{:S(2)}, u32[]{:S(2)}) collective-permute-start(bf16[1,1,8,8,8,512]{5,4,3,2,1,0:T(8,128)(2,1)} %bitcast.243), channel_id=1, source_target_pairs={{16,0},{32,16},{48,32},{64,48},{80,64},{96,80},{112,96},{17,1},{33... | collective-permute-start | bytes 1572872 | tf_op jit(solution)/shard_map/ppermute | solution.py:17
  1.3 70.0 %collective-permute-start = (bf16[1,1,8,8,8,512]{5,4,3,2,1,0:T(8,128)(2,1)}, bf16[1,1,8,8,8,512]{5,4,3,2,1,0:T(8,128)(2,1)S(1)}, u32[]{:S(2)}, u32[]{:S(2)}) collective-permute-start(bf16[1,1,8,8,8,512]{5,4,3,2,1,0:T(8,128)(2,1)} %bitcast.244), channel_id=1, source_target_pairs={{0,16},{16,32},{32,48},{48,64},{64,80},{80,96},{96,112},{1,17},{17... | collective-permute-start | bytes 1572872 | tf_op jit(solution)/shard_map/ppermute | solution.py:16
  6.3 52.1 %copy-start.61 = (s32[8]{0:T(128)}, s32[8]{0:T(128)S(1)}, u32[]{:S(2)}) copy-start(s32[8]{0:T(128)S(1)} %get-tuple-element.8) | copy-start | bytes 100
  6.3 52.1 %copy-start.63 = (s32[8]{0:T(128)}, s32[8]{0:T(128)S(1)}, u32[]{:S(2)}) copy-start(s32[8]{0:T(128)S(1)} %get-tuple-element.16) | copy-start | bytes 100
  6.3 53.9 %copy-start.104 = (s32[8]{0:T(128)}, s32[8]{0:T(128)S(1)}, u32[]{:S(2)}) copy-start(s32[8]{0:T(128)S(1)} %get-tuple-element.12) | copy-start | bytes 100
  6.3 54.5 %copy-start.102 = (s32[8]{0:T(128)}, s32[8]{0:T(128)S(1)}, u32[]{:S(2)}) copy-start(s32[8]{0:T(128)S(1)} %get-tuple-element.19) | copy-start | bytes 100
  6.3 55.1 %copy-start.100 = (s32[8]{0:T(128)}, s32[8]{0:T(128)S(1)}, u32[]{:S(2)}) copy-start(s32[8]{0:T(128)S(1)} %get-tuple-element.14) | copy-start | bytes 100
  6.3 55.7 %copy-start.98 = (s32[8]{0:T(128)}, s32[8]{0:T(128)S(1)}, u32[]{:S(2)}) copy-start(s32[8]{0:T(128)S(1)} %get-tuple-element.18) | copy-start | bytes 100
  17.4 39.7 %copy-start.84 = (s32[8]{0:T(128)}, s32[8]{0:T(128)S(1)}, u32[]{:S(2)}) copy-start(s32[8]{0:T(128)S(1)} %get-tuple-element.32) | copy-start | bytes 100
  17.4 39.7 %copy-start.86 = (s32[8]{0:T(128)}, s32[8]{0:T(128)S(1)}, u32[]{:S(2)}) copy-start(s32[8]{0:T(128)S(1)} %get-tuple-element.33) | copy-start | bytes 100
  17.4 39.7 %copy-start.80 = (s32[8]{0:T(128)}, s32[8]{0:T(128)S(1)}, u32[]{:S(2)}) copy-start(s32[8]{0:T(128)S(1)} %get-tuple-element.34) | copy-start | bytes 100
  17.4 39.8 %copy-start.82 = (s32[8]{0:T(128)}, s32[8]{0:T(128)S(1)}, u32[]{:S(2)}) copy-start(s32[8]{0:T(128)S(1)} %get-tuple-element.35) | copy-start | bytes 100
  17.4 39.8 %copy-start.76 = (s32[8]{0:T(128)}, s32[8]{0:T(128)S(1)}, u32[]{:S(2)}) copy-start(s32[8]{0:T(128)S(1)} %get-tuple-element.36) | copy-start | bytes 100
  17.4 39.8 %copy-start.78 = (s32[8]{0:T(128)}, s32[8]{0:T(128)S(1)}, u32[]{:S(2)}) copy-start(s32[8]{0:T(128)S(1)} %get-tuple-element.37) | copy-start | bytes 100
  71.2 12.0 %copy-start.77 = (s32[8]{0:T(128)S(1)}, s32[8]{0:T(128)}, u32[]{:S(2)}) copy-start(s32[8]{0:T(128)} %copy-done.76) | copy-start | bytes 100
  71.2 12.6 %copy-start.62 = (s32[8]{0:T(128)S(1)}, s32[8]{0:T(128)}, u32[]{:S(2)}) copy-start(s32[8]{0:T(128)} %copy-done.61) | copy-start | bytes 100
  71.2 12.6 %copy-start.64 = (s32[8]{0:T(128)S(1)}, s32[8]{0:T(128)}, u32[]{:S(2)}) copy-start(s32[8]{0:T(128)} %copy-done.63) | copy-start | bytes 100
  72.6 39.2 %collective-permute-start.3 = (bf16[3,1,8,8,8,512]{5,4,3,2,1,0:T(8,128)(2,1)}, bf16[3,1,8,8,8,512]{5,4,3,2,1,0:T(8,128)(2,1)S(1)}, u32[]{:S(2)}, u32[]{:S(2)}) collective-permute-start(bf16[3,1,8,8,8,512]{5,4,3,2,1,0:T(8,128)(2,1)} %pad_maximum_fusion.1), channel_id=1, source_target_pairs={{1,0},{2,1},{3,2},{4,3},{5,4},{6,5},{7,6},{8,7},{9,8},{10,9},{11,1... | collective-permute-start | bytes 4718600 | tf_op jit(solution)/shard_map/ppermute | solution.py:17
  73.9 39.6 %collective-permute-start.2 = (bf16[3,1,8,8,8,512]{5,4,3,2,1,0:T(8,128)(2,1)}, bf16[3,1,8,8,8,512]{5,4,3,2,1,0:T(8,128)(2,1)}, u32[]{:S(2)}, u32[]{:S(2)}) collective-permute-start(bf16[3,1,8,8,8,512]{5,4,3,2,1,0:T(8,128)(2,1)} %pad_maximum_fusion.1), channel_id=1, source_target_pairs={{0,1},{1,2},{2,3},{3,4},{4,5},{5,6},{6,7},{7,8},{8,9},{9,10},{10,1... | collective-permute-start | bytes 4718600 | tf_op jit(solution)/shard_map/ppermute | solution.py:16
  140.0 27.4 %copy-start.19 = (bf16[8,8,8,64]{3,2,1,0:T(8,128)(2,1)S(1)}, bf16[8,8,8,64]{3,2,1,0:T(8,128)(2,1)}, u32[]{:S(2)}) copy-start(bf16[8,8,8,64]{3,2,1,0:T(8,128)(2,1)} %gather_fusion.13) | copy-start | bytes 196612
  140.0 27.4 %copy-start.92 = (pred[8]{0:T(512)(128)(4,1)S(1)}, pred[8]{0:T(512)(128)(4,1)}, u32[]{:S(2)}) copy-start(pred[8]{0:T(512)(128)(4,1)} %get-tuple-element.49) | copy-start | bytes 28
  140.0 27.4 %copy-start.93 = (pred[8]{0:T(512)(128)(4,1)S(1)}, pred[8]{0:T(512)(128)(4,1)}, u32[]{:S(2)}) copy-start(pred[8]{0:T(512)(128)(4,1)} %get-tuple-element.50) | copy-start | bytes 28
  140.0 27.5 %copy-start.125 = (pred[8]{0:T(512)(128)(4,1)S(1)}, pred[8]{0:T(512)(128)(4,1)}, u32[]{:S(2)}) copy-start(pred[8]{0:T(512)(128)(4,1)} %compare_and_fusion.12) | copy-start | bytes 28
  140.0 27.5 %copy-start.126 = (pred[8]{0:T(512)(128)(4,1)S(1)}, pred[8]{0:T(512)(128)(4,1)}, u32[]{:S(2)}) copy-start(pred[8]{0:T(512)(128)(4,1)} %compare_and_fusion.13) | copy-start | bytes 28
  140.0 27.6 %copy-start.70 = (pred[8]{0:T(512)(128)(4,1)S(1)}, pred[8]{0:T(512)(128)(4,1)}, u32[]{:S(2)}) copy-start(pred[8]{0:T(512)(128)(4,1)} %get-tuple-element.51) | copy-start | bytes 28
  140.1 27.6 %copy-start.71 = (pred[8]{0:T(512)(128)(4,1)S(1)}, pred[8]{0:T(512)(128)(4,1)}, u32[]{:S(2)}) copy-start(pred[8]{0:T(512)(128)(4,1)} %get-tuple-element.53) | copy-start | bytes 28
  140.1 27.6 %copy-start.94 = (pred[8]{0:T(512)(128)(4,1)S(1)}, pred[8]{0:T(512)(128)(4,1)}, u32[]{:S(2)}) copy-start(pred[8]{0:T(512)(128)(4,1)} %compare_and_fusion.14) | copy-start | bytes 28
  140.1 27.6 %copy-start.95 = (pred[8]{0:T(512)(128)(4,1)S(1)}, pred[8]{0:T(512)(128)(4,1)}, u32[]{:S(2)}) copy-start(pred[8]{0:T(512)(128)(4,1)} %compare_and_fusion.16) | copy-start | bytes 28
  140.1 27.7 %copy-start.74 = (pred[8]{0:T(512)(128)(4,1)S(1)}, pred[8]{0:T(512)(128)(4,1)}, u32[]{:S(2)}) copy-start(pred[8]{0:T(512)(128)(4,1)} %get-tuple-element.38) | copy-start | bytes 28
  140.1 27.7 %copy-start.75 = (pred[8]{0:T(512)(128)(4,1)S(1)}, pred[8]{0:T(512)(128)(4,1)}, u32[]{:S(2)}) copy-start(pred[8]{0:T(512)(128)(4,1)} %get-tuple-element.54) | copy-start | bytes 28
  140.1 27.7 %copy-start.109 = (pred[8]{0:T(512)(128)(4,1)S(1)}, pred[8]{0:T(512)(128)(4,1)}, u32[]{:S(2)}) copy-start(pred[8]{0:T(512)(128)(4,1)} %compare_and_fusion.8) | copy-start | bytes 28
  140.1 27.7 %copy-start.110 = (pred[8]{0:T(512)(128)(4,1)S(1)}, pred[8]{0:T(512)(128)(4,1)}, u32[]{:S(2)}) copy-start(pred[8]{0:T(512)(128)(4,1)} %compare_and_fusion.17) | copy-start | bytes 28
  (103 other events, 549.3 us)
where the time goes:
time: 226 us; the launch traced here: 224 us
  local copies, waits for them, and re-layouts  88.5 us (39%)
  other arithmetic  62.4 us (28%)
  waiting for transfers between devices  29.1 us (13%)
  blocking collectives  22.3 us (10%)
  starting transfers between devices  11.3 us (5%)
  matrix products  8.01 us (4%)
  between operations  2.61 us (1%)
    gather x26, local copies, waits for them, and re-layouts, shards(): jnp.take(beside_all[:, layer_slice(shift_x), layer_slice(shift_y), depth_...  36.6 us
    ppermute x2, waiting for transfers between devices, extended(): after = lax.ppermute(first, axis, down)  27.4 us
    all_to_all x1, blocking collectives, shards(): lax.all_to_all(outgoing, 'by', split_axis=0, concat_axis=0, tiled=True)  22.3 us
    concatenate x36, local copies, waits for them, and re-layouts, banded_conv(): row_list.append(jnp.concatenate(blocks, 1))  20.8 us
    concatenate x2, other arithmetic, shards(): padded = jnp.concatenate(plane_x, 1)  13.7 us
    and x22, other arithmetic, shards(): jnp.take(beside_all[:, layer_slice(shift_x), layer_slice(shift_y), depth_...  12.5 us
    gather x22, other arithmetic  11.9 us
    another operation x18, local copies, waits for them, and re-layouts, shards(): jnp.take(beside_all[:, layer_slice(shift_x), layer_slice(shift_y), depth_...  10.5 us
  transfers between devices with their start and end apart: 4, of which 2 were waited for; matrix products, arithmetic and copies ran while one was open for 31% of the time, Pallas kernels for 0%

commit v1 on v0

v1 whole, which is shorter than its diff:
```python
import functools

import jax
import jax.numpy as jnp
from jax import lax
from jax.experimental import pallas as pl
from jax.experimental.pallas import tpu as pltpu
from jax.sharding import PartitionSpec as P

MESH = pl.DeviceIdType.MESH
F32 = jnp.float32
BF16 = jnp.bfloat16

EDGE = 8
BRICKS = 8
CH = 64
CO = 128
LANES = EDGE * CH
ROWS = BRICKS * EDGE * EDGE
HALF = 4 * CH
BAND = 6 * CH
FACE = BRICKS * EDGE
MESSAGE = FACE + 2 * BRICKS

T_FACE = BRICKS * EDGE
T_ZERO = T_FACE + 2 * BRICKS
T_SIZE = T_ZERO + EDGE
Y_ZERO = 2 * BRICKS
Y_SIZE = Y_ZERO + 1
E_ZERO = 4 * BRICKS
E_SIZE = E_ZERO + 1

STEPS = (-1, 0, 1)
HALO = [(1, 0), (-1, 0), (0, 1), (0, -1), (1, 1), (1, -1), (-1, 1), (-1, -1)]


def iota(shape, dim):
    return lax.broadcasted_iota(jnp.int32, shape, dim)


def picked_rows():
    row = iota((4 * MESSAGE, ROWS), 0)
    source = iota((4 * MESSAGE, ROWS), 1)
    part, inner = row // MESSAGE, row % MESSAGE
    brick, other = inner // EDGE, inner % EDGE
    face_x = brick * 64 + jnp.where(part == 0, 56, 0) + other
    face_y = inner * 8 + jnp.where(part == 2, 7, 0)
    face = jnp.where(part < 2, face_x, face_y)
    second = inner >= FACE + BRICKS
    edge_x = jnp.where(part == 0, 56, 0) + jnp.where(second, 0, 7)
    edge_y = jnp.where(part == 2, 7, 0) + jnp.where(second, 0, 56)
    edge = other * 64 + jnp.where(part < 2, edge_x, edge_y)
    target = jnp.where(inner < FACE, face, edge)
    return (target == source).astype(F32).astype(BF16)


def repeat_rows(target, corner, first, rows):
    for k in range(BRICKS):
        target[corner, first + k] = jnp.broadcast_to(rows[k : k + 1], (EDGE, LANES))


def kernel(
    size_x, size_y,
    ids_hbm, owner_hbm, feat_hbm, conv_hbm, bias_hbm, down_hbm,
    out_ref,
    ids, owner, feat, conv, bias, down,
    index, sendbuf, xy_recv, edge_recv, table, ytab, etab,
    stack, band, dband, place, hidden, stage,
    load_sem, halo_send, halo_recv, out_send, out_recv, own_sem,
):
    i = lax.axis_index("bx")
    j = lax.axis_index("by")

    def beside(step_x, step_y):
        return (lax.rem(i + step_x + size_x, size_x), lax.rem(j + step_y + size_y, size_y))

    barrier = pltpu.get_barrier_semaphore()
    others = [(sx, sy) for sx, sy in HALO if sx != 0]
    for sx, sy in others:
        pl.semaphore_signal(barrier, inc=1, device_id=beside(sx, sy), device_id_type=MESH)
    for d in range(1, size_y):
        pl.semaphore_signal(barrier, inc=1, device_id=beside(0, d), device_id_type=MESH)

    loads = [
        pltpu.make_async_copy(source, target, load_sem.at[k])
        for k, (source, target) in enumerate(
            [
                (feat_hbm, feat),
                (conv_hbm, conv),
                (ids_hbm, ids),
                (owner_hbm, owner),
                (bias_hbm, bias),
                (down_hbm, down),
            ]
        )
    ]
    for load in loads:
        load.start()

    pick = picked_rows()
    loads[0].wait()
    picked = jnp.dot(pick, feat[...], preferred_element_type=F32)
    packed = picked.astype(BF16)
    for k in range(4):
        sendbuf[k] = packed[k * MESSAGE : (k + 1) * MESSAGE]

    pl.semaphore_wait(barrier, len(others) + size_y - 1)
    copies = []
    for k, (sx, sy) in enumerate(HALO):
        if k < 4:
            source, target = sendbuf.at[k], xy_recv.at[k]
        else:
            source = sendbuf.at[(k - 4) // 2, pl.ds(FACE, 16)]
            target = edge_recv.at[k - 4]
        copy = pltpu.make_async_remote_copy(
            src_ref=source,
            dst_ref=target,
            send_sem=halo_send.at[k],
            recv_sem=halo_recv.at[k],
            device_id=beside(sx, sy),
            device_id_type=MESH,
        )
        copy.start()
        copies.append(copy)

    table[0:T_FACE] = feat[...].astype(F32).reshape(T_FACE, EDGE, LANES)
    table[T_ZERO:T_SIZE] = jnp.zeros((EDGE, EDGE, LANES), F32)
    for k in range(2):
        face = picked[(2 + k) * MESSAGE : (2 + k) * MESSAGE + FACE]
        ytab[k, 0:BRICKS] = face.reshape(BRICKS, EDGE, LANES)
        ytab[k, Y_ZERO] = jnp.zeros((EDGE, LANES), F32)
    for k in range(4):
        first = k // 2 * MESSAGE + FACE + k % 2 * BRICKS
        repeat_rows(etab, k, 0, picked[first : first + BRICKS])
        etab[k, E_ZERO] = jnp.zeros((EDGE, LANES), F32)

    loads[2].wait()
    for g in range(BRICKS):
        for tap in range(27):
            sx, sy = tap // 9 - 1, tap // 3 % 3 - 1
            value = ids[g, tap]
            brick = value & 7
            far_x = jnp.where(value >> 3 >> 4 == i, 0, 1)
            far_y = jnp.where((value >> 3) & 15 == j, 0, 1)
            if sx == 0 and sy == 0:
                row, zero = brick * EDGE, T_ZERO
            elif sy == 0:
                edge_x, side = (7, 0) if sx < 0 else (0, 1)
                row = jnp.where(far_x == 0, brick * EDGE + edge_x, T_FACE + side * BRICKS + brick)
                zero = T_ZERO
            elif sx == 0:
                row, zero = far_y * BRICKS + brick, Y_ZERO
            else:
                row, zero = far_x * 16 + far_y * 8 + brick, E_ZERO
            index[g, tap] = jnp.where(value >= 0, row, zero)

    loads[1].wait()
    empty = jnp.zeros((CH, CH), BF16)
    blank = jnp.zeros((CH, 2 * CH), BF16)
    for ty in range(3):
        for tx in range(3):
            w = [conv[tx * 9 + ty * 3 + tz] for tz in range(3)]
            pairs = {
                -1: jnp.concatenate([w[0], empty], 1),
                0: jnp.concatenate([w[1], w[0]], 1),
                1: jnp.concatenate([w[2], w[1]], 1),
                2: jnp.concatenate([empty, w[2]], 1),
            }
            for place_in, depth_in in enumerate((0, 1, 2, 3, 4, -1)):
                for q in range(2):
                    first = tx * BAND + place_in * CH
                    band[ty, first : first + CH, q * 128 : (q + 1) * 128] = pairs.get(
                        depth_in - 2 * q, blank
                    )
    loads[5].wait()
    for a in range(2):
        for z in range(4):
            for b in range(2):
                for half in range(2):
                    first = b * 256 + half * 128
                    block = down[a * 4 + b * 2 + z % 2] if z // 2 == half else blank
                    dband[a, z * CH : (z + 1) * CH, first : first + 128] = block

    loads[3].wait()
    owners = [owner[g, 0] for g in range(BRICKS)]
    slots = []
    for g in range(BRICKS):
        rank = jnp.int32(0)
        for earlier in range(g):
            rank = rank + jnp.where(owners[earlier] == owners[g], 1, 0)
        slots.append(owners[g] * 2 + rank)
    col = iota((16, 256), 1)
    xy = iota((16, 256), 0)
    slot_of = jnp.zeros((16, 256), jnp.int32)
    for g in range(BRICKS):
        slot_of = jnp.where(col // 8 % 8 == g, slots[g], slot_of)
    slot_of = jnp.where((col // 64 == xy // 4) & (col % 8 == xy % 4 * 2), slot_of, -1)
    for s in range(2 * size_y):
        place[s * 16 : (s + 1) * 16] = (slot_of == s).astype(F32).astype(BF16)

    loads[4].wait()
    for copy in copies:
        copy.wait()
    for k in range(2):
        over_x = xy_recv[k].astype(F32)
        over_y = xy_recv[2 + k].astype(F32)
        first = T_FACE + k * BRICKS
        table[first : first + BRICKS] = over_x[0:FACE].reshape(BRICKS, EDGE, LANES)
        ytab[k, BRICKS : 2 * BRICKS] = over_y[0:FACE].reshape(BRICKS, EDGE, LANES)
        for side in range(2):
            first = FACE + side * BRICKS
            repeat_rows(etab, side * 2 + k, 8, over_y[first : first + BRICKS])
            repeat_rows(etab, k * 2 + side, 16, over_x[first : first + BRICKS])
            diagonal = edge_recv[k * 2 + side].astype(F32)
            diagonal = diagonal[side * BRICKS : (side + 1) * BRICKS]
            repeat_rows(etab, k * 2 + side, 24, diagonal)

    low = iota((EDGE, 128), 1) < CH
    last_row = iota((EDGE, BAND), 0) == 7
    first_row = iota((EDGE, BAND), 0) == 0

    def halves(read, centre, minus, plus):
        c = read(centre, 0, LANES)
        m = read(minus, LANES - 128, LANES)
        p = read(plus, 0, 128)
        e0 = jnp.where(low, c[:, 256:384], m)
        e1 = jnp.where(low, p, c[:, 128:256])
        return (
            jnp.concatenate([c[:, 0:256], e0], 1),
            jnp.concatenate([c[:, 256:512], e1], 1),
        )

    def one_slab(g, x):
        sx = -1 if x < 0 else (1 if x > 7 else 0)
        shift = x if sx == 0 else 0
        result = []
        for sy in STEPS:
            tap = (sx + 1) * 9 + (sy + 1) * 3
            if sy == 0:
                def read(row, low_lane, high_lane):
                    return table[row + shift, :, low_lane:high_lane]
            elif sx == 0:
                def read(row, low_lane, high_lane, side=(sy + 1) // 2):
                    lines = ytab[side, row, :, low_lane:high_lane]
                    return pltpu.roll(lines, (7 - x if side == 0 else 0 - x) & 7, 0)
            else:
                def read(row, low_lane, high_lane, corner=(sx + 1) // 2 * 2 + (sy + 1) // 2):
                    return etab[corner, row, :, low_lane:high_lane]
            result.append(halves(read, index[g, tap + 1], index[g, tap], index[g, tap + 2]))
        before, same, after = result
        return [
            [jnp.where(last_row, before[h], same[h]), same[h], jnp.where(first_row, after[h], same[h])]
            for h in range(2)
        ]

    def gather(pair, carry):
        for x in range(-1, 9):
            even = one_slab(pair * 2, x)
            odd = one_slab(pair * 2 + 1, x)
            for h in range(2):
                for ty in range(3):
                    both = jnp.concatenate([even[h][ty], odd[h][ty]], 0).astype(BF16)
                    stack[ty, x + 1, h, pl.ds(pl.multiple_of(pair * 16, 16), 16)] = both
        return carry

    lax.fori_loop(0, BRICKS // 2, gather, 0)

    bias_row = jnp.concatenate([bias[...]] * 4, 1)
    sends = []
    for h in range(2):
        total = None
        for ty in range(3):
            window = jnp.concatenate(
                [stack[ty, tx : tx + 8, h].reshape(ROWS, BAND) for tx in range(3)], 1
            )
            part = jnp.dot(window, band[ty], preferred_element_type=F32)
            if ty != 1:
                part = pltpu.roll(part.reshape(64, 8, HALF), 1 if ty == 0 else 7, 1)
                part = part.reshape(ROWS, HALF)
            total = part if total is None else total + part
        v = total + bias_row
        own = stack[1, 1:9, h, :, 0:HALF].reshape(ROWS, HALF).astype(F32)
        act = 0.5 * v * (1.0 + jnp.tanh(0.5 * v))
        hidden[...] = (own + act).astype(BF16).reshape(4, 2, 64, HALF)
        coarse = jnp.dot(
            hidden[:, 0].reshape(256, HALF), dband[0], preferred_element_type=F32
        ) + jnp.dot(hidden[:, 1].reshape(256, HALF), dband[1], preferred_element_type=F32)
        odd_rows = pltpu.roll(coarse[:, 256:].reshape(32, 8, 256), 7, 1).reshape(256, 256)
        coarse = (coarse[:, :256] + odd_rows).astype(BF16)
        placed = jnp.dot(place[...], coarse, preferred_element_type=F32).astype(BF16)
        lanes = pl.ds(h * 256, 256)
        stage[:, :, h * 256 : (h + 1) * 256] = placed.reshape(2 * size_y, 16, 256)
        for d in range(1, size_y):
            dest = lax.rem(j + d, size_y)
            copy = pltpu.make_async_remote_copy(
                src_ref=stage.at[pl.ds(dest * 2, 2), :, lanes],
                dst_ref=out_ref.at[pl.ds(j * 2, 2), :, lanes],
                send_sem=out_send.at[h, d],
                recv_sem=out_recv.at[h, d],
                device_id=(i, dest),
                device_id_type=MESH,
            )
            copy.start()
            sends.append(copy)
        copy = pltpu.make_async_copy(
            stage.at[pl.ds(j * 2, 2), :, lanes], out_ref.at[pl.ds(j * 2, 2), :, lanes], own_sem.at[h]
        )
        copy.start()
        sends.append(copy)
    for copy in sends:
        copy.wait()


def shards(features, neighbour_ids, conv_weight, conv_bias, down_weight, coarse_owner):
    size_x = lax.axis_size("bx")
    size_y = lax.axis_size("by")
    slots = 2 * size_y
    any_spec = pl.BlockSpec(memory_space=pl.ANY)
    out = pl.pallas_call(
        functools.partial(kernel, size_x, size_y),
        out_shape=jax.ShapeDtypeStruct((slots, 16, 4 * CO), BF16),
        in_specs=[any_spec] * 6,
        out_specs=any_spec,
        scratch_shapes=[
            pltpu.SMEM((BRICKS, 27), jnp.int32),
            pltpu.SMEM((BRICKS, 1), jnp.int32),
            pltpu.VMEM((ROWS, LANES), BF16),
            pltpu.VMEM((27, CH, CH), BF16),
            pltpu.VMEM((1, CH), F32),
            pltpu.VMEM((8, CH, CO), BF16),
            pltpu.SMEM((BRICKS, 27), jnp.int32),
            pltpu.VMEM((4, MESSAGE, LANES), BF16),
            pltpu.VMEM((4, MESSAGE, LANES), BF16),
            pltpu.VMEM((4, 16, LANES), BF16),
            pltpu.VMEM((T_SIZE, EDGE, LANES), F32),
            pltpu.VMEM((2, Y_SIZE, EDGE, LANES), F32),
            pltpu.VMEM((4, E_SIZE, EDGE, LANES), F32),
            pltpu.VMEM((3, 10, 2, FACE, BAND), BF16),
            pltpu.VMEM((3, 3 * BAND, HALF), BF16),
            pltpu.VMEM((2, HALF, 512), BF16),
            pltpu.VMEM((16 * slots, 256), BF16),
            pltpu.VMEM((4, 2, FACE, HALF), BF16),
            pltpu.VMEM((slots, 16, 4 * CO), BF16),
            pltpu.SemaphoreType.DMA((6,)),
            pltpu.SemaphoreType.DMA((8,)),
            pltpu.SemaphoreType.DMA((8,)),
            pltpu.SemaphoreType.DMA((2, 16)),
            pltpu.SemaphoreType.DMA((2, 16)),
            pltpu.SemaphoreType.DMA((2,)),
        ],
        compiler_params=pltpu.CompilerParams(
            collective_id=0, has_side_effects=True, vmem_limit_bytes=48 * 1024 * 1024
        ),
        name="brick_encoder",
    )(
        neighbour_ids,
        coarse_owner,
        features.reshape(ROWS, LANES),
        conv_weight,
        conv_bias.reshape(1, CH),
        down_weight,
    )
    return out.reshape(slots, 4, 4, 4 * CO)


def solution(mesh):
    in_specs = (
        P(("bx", "by"), None, None, None),
        P(("bx", "by"), None),
        P(),
        P(),
        P(),
        P(("bx", "by"), None),
    )
    out_specs = P(("bx", "by"), None, None, None)
    return jax.shard_map(shards, mesh=mesh, in_specs=in_specs, out_specs=out_specs, check_vma=False)
```

time: 226 us -> 29.7 us (0.13)
  local copies, waits for them, and re-layouts: 88.5 us -> 4.64 us
  other arithmetic: 62.4 us -> 0 us
  waiting for transfers between devices: 29.1 us -> 0 us
  Pallas kernels: 0 us -> 24.6 us
  blocking collectives: 22.3 us -> 0 us
  starting transfers between devices: 11.3 us -> 0 us
  matrix products: 8.01 us -> 0 us
  between operations: 2.61 us -> 0.01 us
    gather x26 -> x0, local copies, waits for them, and re-layouts: 36.6 us -> none  [shards(): jnp.take(beside_all[:, layer_slice(shift_x), layer_slice(shift_y), depth_...]
    ppermute x4 -> x0, waiting for transfers between devices: 29.1 us -> none  [the longest x2 27.4 us: extended(): after = lax.ppermute(first, axis, down)]
    pallas_call x0 -> x1, Pallas kernels: none -> 24.6 us  [shards(): pl.pallas_call(functools.partial(kernel, size_x, size_y), out_shape=jax.S...]
    concatenate x44 -> x0, local copies, waits for them, and re-layouts: 23.9 us -> none  [the longest x36 20.8 us: banded_conv(): row_list.append(jnp.concatenate(blocks, 1))]
    all_to_all x1 -> x0, blocking collectives: 22.3 us -> none  [shards(): lax.all_to_all(outgoing, 'by', split_axis=0, concat_axis=0, tiled=True)]
    concatenate x4 -> x0, other arithmetic: 16.7 us -> none  [the longest x2 13.7 us: shards(): padded = jnp.concatenate(plane_x, 1)]
    select_n x44 -> x0, other arithmetic: 16.4 us -> none  [the longest x18 8.9 us: shards(): jnp.where(present[:, column][:, None, None, None], taken, jnp.zeros((), t...]
    and x22 -> x0, other arithmetic: 12.5 us -> none  [shards(): jnp.take(beside_all[:, layer_slice(shift_x), layer_slice(shift_y), depth_...]
  transfers between devices with their start and end apart: 4 -> 0, of which waited for: 2 -> 0; matrix products, arithmetic and copies ran while one was open for 31% -> 0% of each run, Pallas kernels for 0% -> 0%
where the time goes in v1:
time: 29.7 us; the launch traced here: 29.3 us
  Pallas kernels  24.6 us (83%)
  local copies, waits for them, and re-layouts  4.64 us (16%)
    pallas_call x1, Pallas kernels, shards(): pl.pallas_call(functools.partial(kernel, size_x, size_y), out_shape=jax.S...  24.6 us
    unnamed x11, local copies, waits for them, and re-layouts  3.72 us
    reshape x1, local copies, waits for them, and re-layouts, shards(): return out.reshape(slots, 4, 4, 4 * CO)  0.92 us

profile of v1, /device:TPU:0, one launch (start us, length us, event | category | flops | bytes accessed | tf_op | source)
XLA Modules:
  0.0 29.3 jit_solution(6778801520888332267)
XLA Ops:
  0.0 0.0 copy-start.3
  0.0 0.0 copy-start.4
  0.0 0.8 %copy.7.owner_hbm = s32[8,1]{1,0:T(8,128)S(1)} copy(s32[8,1]{0,1:T(1,128)} %param.11) | data formatting | bytes 64 | tf_op args[5]
  0.8 0.0 copy-done.3
  0.8 0.0 copy-done.4
  0.8 0.0 copy-start
  0.8 1.0 %copy-done = bf16[8,8,8,512]{3,2,1,0:T(8,128)(2,1)S(1)} copy-done((bf16[8,8,8,512]{3,2,1,0:T(8,128)(2,1)S(1)}, bf16[8,8,8,512]{3,2,1,0:T(8,128)(2,1)}, u32[]{:S(2)}) %copy-start) | copy-done | bytes 524312
  1.8 0.0 copy-start.1
  1.8 1.0 %copy-done.1 = bf16[27,64,64]{2,1,0:T(8,128)(2,1)S(1)} copy-done((bf16[27,64,64]{2,1,0:T(8,128)(2,1)S(1)}, bf16[27,64,64]{2,1,0:T(8,128)(2,1)}, u32[]{:S(2)}) %copy-start.1) | copy-done | bytes 221208
  2.8 0.0 copy-start.2
  2.8 0.9 %copy-done.2 = bf16[8,64,128]{2,1,0:T(8,128)(2,1)S(1)} copy-done((bf16[8,64,128]{2,1,0:T(8,128)(2,1)S(1)}, bf16[8,64,128]{2,1,0:T(8,128)(2,1)}, u32[]{:S(2)}) %copy-start.2) | copy-done | bytes 131096
  3.7 24.6 %brick_encoder.1 = bf16[32,16,512]{2,1,0:T(8,128)(2,1)S(1)} custom-call(s32[8,27]{1,0:T(8,128)S(1)} %copy-done.3, s32[8,1]{1,0:T(8,128)S(1)} %copy.7.owner_hbm, bf16[512,512]{1,0:T(8,128)(2,1)S(1)} %bitcast.2, bf16[27,64,64]{2,1,0:T(8,128)(2,1)S(1)} %copy-done.1, f32[1,64]{1,0:T(1,128)S(1)} %bitcast.3, bf16[8,64,128]{2,1,0:T(8,128)(2,1)S(1)} %copy-done.2), custom_call_target="tpu_custom_call" | custom-call | tf_op jit(solution)/shard_map/brick_encoder/pallas_call | solution.py:319
  28.4 0.9 %reshape.11 = bf16[32,4,4,512]{3,2,1,0:T(4,128)(2,1)} reshape(bf16[32,16,512]{2,1,0:T(8,128)(2,1)S(1)} %brick_encoder.1) | data formatting | bytes 1048576 | tf_op jit(solution)/shard_map/reshape | solution.py:363
Async XLA Ops:
  0.0 0.8 %copy-start.3 = (s32[8,27]{1,0:T(8,128)S(1)}, s32[8,27]{1,0:T(8,128)}, u32[]{:S(2)}) copy-start(s32[8,27]{1,0:T(8,128)} %ids_hbm.1) | copy-start | bytes 2596
  0.0 0.8 %copy-start.4 = (f32[64]{0:T(128)S(1)}, f32[64]{0:T(128)}, u32[]{:S(2)}) copy-start(f32[64]{0:T(128)} %param.9) | copy-start | bytes 772
  0.8 1.0 %copy-start = (bf16[8,8,8,512]{3,2,1,0:T(8,128)(2,1)S(1)}, bf16[8,8,8,512]{3,2,1,0:T(8,128)(2,1)}, u32[]{:S(2)}) copy-start(bf16[8,8,8,512]{3,2,1,0:T(8,128)(2,1)} %param.6) | copy-start | bytes 1572868
  1.8 1.0 %copy-start.1 = (bf16[27,64,64]{2,1,0:T(8,128)(2,1)S(1)}, bf16[27,64,64]{2,1,0:T(8,128)(2,1)}, u32[]{:S(2)}) copy-start(bf16[27,64,64]{2,1,0:T(8,128)(2,1)} %conv_hbm.1) | copy-start | bytes 663556
  2.8 0.9 %copy-start.2 = (bf16[8,64,128]{2,1,0:T(8,128)(2,1)S(1)}, bf16[8,64,128]{2,1,0:T(8,128)(2,1)}, u32[]{:S(2)}) copy-start(bf16[8,64,128]{2,1,0:T(8,128)(2,1)} %down_hbm.1) | copy-start | bytes 393220

commit v2 on v1

v2 whole, which is shorter than its diff:
```python
import functools

import jax
import jax.numpy as jnp
from jax import lax
from jax.experimental import pallas as pl
from jax.experimental.pallas import tpu as pltpu
from jax.sharding import PartitionSpec as P

MESH = pl.DeviceIdType.MESH
F32 = jnp.float32
BF16 = jnp.bfloat16

EDGE = 8
BRICKS = 8
CH = 64
CO = 128
LANES = EDGE * CH
ROWS = BRICKS * EDGE * EDGE
HALF = 4 * CH
BAND = 6 * CH
FACE = BRICKS * EDGE
MESSAGE = FACE + 2 * BRICKS

T_FACE = BRICKS * EDGE
T_ZERO = T_FACE + 2 * BRICKS
T_SIZE = T_ZERO + EDGE
Y_ZERO = 2 * BRICKS
Y_SIZE = Y_ZERO + 1
E_ZERO = 4 * BRICKS
E_SIZE = E_ZERO + 1

STEPS = (-1, 0, 1)
SIDE = 4
HALO = [(1, 0), (-1, 0), (0, 1), (0, -1), (1, 1), (1, -1), (-1, 1), (-1, -1)]


def iota(shape, dim):
    return lax.broadcasted_iota(jnp.int32, shape, dim)


def picked_rows(message):
    inner = iota((MESSAGE, 128), 0)
    lane = iota((MESSAGE, 128), 1)
    brick, other = inner >> 3, inner & 7
    second = inner >= FACE + BRICKS
    if message < 2:
        at = 56 if message == 0 else 0
        face = brick * 64 + at + other
        edge = other * 64 + at + jnp.where(second, 0, 7)
    else:
        at = 7 if message == 2 else 0
        face = inner * 8 + at
        edge = other * 64 + at + jnp.where(second, 0, 56)
    target = jnp.where(inner < FACE, face, edge) - lane
    blocks = [(target == 128 * k).astype(F32) for k in range(ROWS // 128)]
    return jnp.concatenate(blocks, 1).astype(BF16)


def repeat_rows(target, corner, first, rows):
    for k in range(BRICKS):
        target[corner, first + k] = jnp.broadcast_to(rows[k : k + 1], (EDGE, LANES))


def kernel(
    size_x, size_y,
    ids_hbm, owner_hbm, feat_hbm, conv_hbm, bias_hbm, down_hbm,
    out_ref,
    ids, owner, feat, conv, bias, down,
    index, sendbuf, xy_recv, edge_recv, table, ytab, etab,
    stack, band, dband, named, place, raw, relay, ready,
    load_sem, halo_send, halo_recv, name_send, name_recv,
    raw_send, raw_recv, out_send, out_recv, own_sem,
):
    i = lax.axis_index("bx")
    j = lax.axis_index("by")
    z, y = j // SIDE, j % SIDE

    loads = [
        pltpu.make_async_copy(source, target, load_sem.at[k])
        for k, (source, target) in enumerate(
            [
                (feat_hbm, feat),
                (conv_hbm, conv),
                (ids_hbm, ids),
                (owner_hbm, owner),
                (bias_hbm, bias),
                (down_hbm, down),
            ]
        )
    ]
    for load in loads:
        load.start()

    def beside(step_x, step_y):
        return (lax.rem(i + step_x + size_x, size_x), lax.rem(j + step_y + size_y, size_y))

    def partner(h, d):
        if h == 0:
            return (i, z * SIDE + lax.rem(y + d, SIDE))
        return (i, lax.rem(z + d, SIDE) * SIDE + y)

    barrier = pltpu.get_barrier_semaphore()
    greeted = [beside(sx, sy) for sx, sy in HALO]
    greeted += [partner(h, d) for h in range(2) for d in range(1, SIDE)]
    for device in greeted:
        pl.semaphore_signal(barrier, inc=1, device_id=device, device_id_type=MESH)

    def remote(source, target, send_sem, recv_sem, device):
        copy = pltpu.make_async_remote_copy(
            src_ref=source,
            dst_ref=target,
            send_sem=send_sem,
            recv_sem=recv_sem,
            device_id=device,
            device_id_type=MESH,
        )
        copy.start()
        return copy

    picks = [picked_rows(k) for k in range(4)]
    loads[0].wait()
    picked = []
    for k in range(4):
        picked.append(jnp.dot(picks[k], feat[...], preferred_element_type=F32))
        sendbuf[k] = picked[k].astype(BF16)

    pl.semaphore_wait(barrier, len(greeted))
    copies = []
    for k, (sx, sy) in enumerate(HALO):
        if k < 4:
            source, target = sendbuf.at[k], xy_recv.at[k]
        else:
            source = sendbuf.at[(k - 4) // 2, pl.ds(FACE, 16)]
            target = edge_recv.at[k - 4]
        copies.append(
            remote(source, target, halo_send.at[k], halo_recv.at[k], beside(sx, sy))
        )

    loads[3].wait()
    owners = [owner[0, g] for g in range(BRICKS)]
    lane = iota((EDGE, 128), 1)
    slot_of = jnp.zeros((EDGE, 128), jnp.int32)
    for g in range(BRICKS):
        rank = jnp.int32(0)
        for earlier in range(g):
            rank = rank + jnp.where(owners[earlier] == owners[g], 1, 0)
        slot_of = jnp.where(lane // 16 == g, owners[g] * 2 + rank, slot_of)
    named[0, 0] = slot_of.astype(F32)
    name_copies = [
        remote(named.at[0, 0], named.at[h, d], name_send.at[h, d], name_recv.at[h, d], partner(h, d))
        for h in range(2)
        for d in range(1, SIDE)
    ]

    table[0:T_FACE] = feat[...].astype(F32).reshape(T_FACE, EDGE, LANES)
    table[T_ZERO:T_SIZE] = jnp.zeros((EDGE, EDGE, LANES), F32)
    for k in range(2):
        ytab[k, 0:BRICKS] = picked[2 + k][0:FACE].reshape(BRICKS, EDGE, LANES)
        ytab[k, Y_ZERO] = jnp.zeros((EDGE, LANES), F32)
    for k in range(4):
        first = FACE + k % 2 * BRICKS
        repeat_rows(etab, k, 0, picked[k // 2][first : first + BRICKS])
        etab[k, E_ZERO] = jnp.zeros((EDGE, LANES), F32)

    loads[2].wait()
    for g in range(BRICKS):
        for tap in range(27):
            sx, sy = tap // 9 - 1, tap // 3 % 3 - 1
            value = ids[g, tap]
            brick = value & 7
            far_x = jnp.where(value >> 3 >> 4 == i, 0, 1)
            far_y = jnp.where((value >> 3) & 15 == j, 0, 1)
            if sx == 0 and sy == 0:
                row, zero = brick * EDGE, T_ZERO
            elif sy == 0:
                edge_x, side = (7, 0) if sx < 0 else (0, 1)
                row = jnp.where(far_x == 0, brick * EDGE + edge_x, T_FACE + side * BRICKS + brick)
                zero = T_ZERO
            elif sx == 0:
                row, zero = far_y * BRICKS + brick, Y_ZERO
            else:
                row, zero = far_x * 16 + far_y * 8 + brick, E_ZERO
            index[g, tap] = jnp.where(value >= 0, row, zero)

    loads[1].wait()
    empty = jnp.zeros((CH, CH), BF16)
    blank = jnp.zeros((CH, 2 * CH), BF16)
    for ty in range(3):
        for tx in range(3):
            w = [conv[tx * 9 + ty * 3 + tz] * jnp.array(0.5, BF16) for tz in range(3)]
            pairs = {
                -1: jnp.concatenate([w[0], empty], 1),
                0: jnp.concatenate([w[1], w[0]], 1),
                1: jnp.concatenate([w[2], w[1]], 1),
                2: jnp.concatenate([empty, w[2]], 1),
            }
            for place_in, depth_in in enumerate((0, 1, 2, 3, 4, -1)):
                for q in range(2):
                    first = tx * BAND + place_in * CH
                    band[ty, first : first + CH, q * 128 : (q + 1) * 128] = pairs.get(
                        depth_in - 2 * q, blank
                    )
    loads[5].wait()
    for a in range(2):
        for k in range(4):
            for b in range(2):
                for half in range(2):
                    first = b * 256 + half * 128
                    block = down[a * 4 + b * 2 + k % 2] if k // 2 == half else blank
                    dband[a * HALF + k * CH : a * HALF + (k + 1) * CH, first : first + 128] = block

    for copy in name_copies:
        copy.wait()
    same_xy = iota((16, 128), 0) == (iota((16, 128), 1) & 15)
    for h in range(2):
        for d in range(SIDE):
            slots = named[h, d] if d else named[0, 0]
            slots = jnp.where(same_xy, jnp.concatenate([slots, slots], 0), -1.0)
            for far in range(SIDE):
                device = far * SIDE + y if h == 0 else z * SIDE + far
                for rank in range(2):
                    wanted = (device * 2 + rank).astype(F32)
                    first = (far * 2 + rank) * 16
                    place[h, d, first : first + 16] = (slots == wanted).astype(F32).astype(BF16)

    loads[4].wait()
    for copy in copies:
        copy.wait()
    for k in range(2):
        over_x = xy_recv[k].astype(F32)
        over_y = xy_recv[2 + k].astype(F32)
        first = T_FACE + k * BRICKS
        table[first : first + BRICKS] = over_x[0:FACE].reshape(BRICKS, EDGE, LANES)
        ytab[k, BRICKS : 2 * BRICKS] = over_y[0:FACE].reshape(BRICKS, EDGE, LANES)
        for side in range(2):
            first = FACE + side * BRICKS
            repeat_rows(etab, side * 2 + k, 8, over_y[first : first + BRICKS])
            repeat_rows(etab, k * 2 + side, 16, over_x[first : first + BRICKS])
            diagonal = edge_recv[k * 2 + side].astype(F32)
            diagonal = diagonal[side * BRICKS : (side + 1) * BRICKS]
            repeat_rows(etab, k * 2 + side, 24, diagonal)

    low = iota((EDGE, 128), 1) < CH
    last_row = iota((EDGE, BAND), 0) == 7
    first_row = iota((EDGE, BAND), 0) == 0

    def halves(read, centre, minus, plus):
        c = read(centre, 0, LANES)
        m = read(minus, LANES - 128, LANES)
        p = read(plus, 0, 128)
        e0 = jnp.where(low, c[:, 256:384], m)
        e1 = jnp.where(low, p, c[:, 128:256])
        return (
            jnp.concatenate([c[:, 0:256], e0], 1),
            jnp.concatenate([c[:, 256:512], e1], 1),
        )

    def one_slab(g, x):
        sx = -1 if x < 0 else (1 if x > 7 else 0)
        shift = x if sx == 0 else 0
        result = []
        for sy in STEPS:
            tap = (sx + 1) * 9 + (sy + 1) * 3
            if sy == 0:
                def read(row, low_lane, high_lane):
                    return table[row + shift, :, low_lane:high_lane]
            elif sx == 0:
                def read(row, low_lane, high_lane, side=(sy + 1) // 2):
                    lines = ytab[side, row, :, low_lane:high_lane]
                    return pltpu.roll(lines, (7 - x if side == 0 else 0 - x) & 7, 0)
            else:
                def read(row, low_lane, high_lane, corner=(sx + 1) // 2 * 2 + (sy + 1) // 2):
                    return etab[corner, row, :, low_lane:high_lane]
            result.append(halves(read, index[g, tap + 1], index[g, tap], index[g, tap + 2]))
        before, same, after = result
        return [
            [jnp.where(last_row, before[h], same[h]), same[h], jnp.where(first_row, after[h], same[h])]
            for h in range(2)
        ]

    def gather(pair, slabs):
        for x in slabs:
            even = one_slab(pair * 2, x)
            odd = one_slab(pair * 2 + 1, x)
            for h in range(2):
                for ty in range(3):
                    both = jnp.concatenate([even[h][ty], odd[h][ty]], 0)
                    stack[pair, ty, x + 1, h] = both.astype(BF16)

    bias_row = jnp.concatenate([bias[...] * 0.5] * 4, 1)
    row, col = iota((32, 64), 0), iota((32, 64), 1)
    even_rows = ((row & 15) >> 2) * 16 + (row >> 4) * 8 + (row & 3) * 2 == col
    even_rows = even_rows.astype(F32).astype(BF16)
    pairs = BRICKS // 2
    parts = [range(-1, 3), range(3, 6), range(6, 9)]
    raw_copies = []
    gather(0, range(-1, 9))
    for pair in range(pairs):
        total = None
        for ty in range(3):
            window = jnp.concatenate(
                [stack[pair, ty, tx : tx + 8].reshape(256, BAND) for tx in range(3)], 1
            )
            part = jnp.dot(window, band[ty], preferred_element_type=F32)
            if ty != 1:
                part = pltpu.roll(part.reshape(32, 8, HALF), 1 if ty == 0 else 7, 1)
                part = part.reshape(256, HALF)
            total = part if total is None else total + part
            if pair + 1 < pairs:
                gather(pair + 1, parts[ty])
        half_v = total + bias_row
        own = stack[pair, 1, 1:9, :, :, 0:HALF].reshape(256, HALF).astype(F32)
        hidden = (own + (half_v + half_v * jnp.tanh(half_v))).astype(BF16)
        hidden = hidden.reshape(4, 2, 32, HALF)
        hidden = jnp.concatenate(
            [hidden[:, 0].reshape(128, HALF), hidden[:, 1].reshape(128, HALF)], 1
        )
        coarse = jnp.dot(hidden, dband[...], preferred_element_type=F32)
        odd = pltpu.roll(coarse[:, 256:].reshape(16, 8, 256), 7, 1).reshape(128, 256)
        coarse = (coarse[:, :256] + odd).astype(BF16).reshape(4, 2, 16, 256)
        for h in range(2):
            piece = jnp.dot(
                even_rows, coarse[:, h].reshape(64, 256), preferred_element_type=F32
            )
            raw[h, pair * 2 : pair * 2 + 2] = piece.astype(BF16).reshape(2, 16, 256)
        if pair % 2 == 1:
            some = pl.ds(pair * 2 - 2, 4)
            for h in range(2):
                for d in range(1, SIDE):
                    raw_copies.append(
                        remote(
                            raw.at[h, some],
                            relay.at[h, d, some],
                            raw_send.at[h, pair // 2, d],
                            raw_recv.at[h, pair // 2, d],
                            partner(h, d),
                        )
                    )

    def forward(h, d):
        pieces = raw[h] if d == 0 else relay[h, d]
        placed = jnp.dot(
            place[h, d], pieces.reshape(128, 256), preferred_element_type=F32
        ).astype(BF16)
        source = lax.rem((y if h == 0 else z) - d + SIDE, SIDE)
        ready[h, :, source] = placed.reshape(SIDE, 2, 16, 256)

    for h in range(2):
        forward(h, 0)
    for copy in raw_copies:
        copy.wait()
    out_copies = []
    for h in range(2):
        for d in range(1, SIDE):
            forward(h, d)
        lanes = pl.ds(h * 256, 256)
        target = out_ref.at[z, :, :, :, lanes] if h == 0 else out_ref.at[:, y, :, :, lanes]
        here = z if h == 0 else y
        for d in range(1, SIDE):
            out_copies.append(
                remote(
                    ready.at[h, lax.rem(here + d, SIDE)],
                    target,
                    out_send.at[h, d],
                    out_recv.at[h, d],
                    partner(1 - h, d),
                )
            )
        copy = pltpu.make_async_copy(ready.at[h, here], target, own_sem.at[h])
        copy.start()
        out_copies.append(copy)
    for copy in out_copies:
        copy.wait()


def shards(features, neighbour_ids, conv_weight, conv_bias, down_weight, coarse_owner):
    size_x = lax.axis_size("bx")
    size_y = lax.axis_size("by")
    slots = 2 * size_y
    hbm_spec = pl.BlockSpec(memory_space=pltpu.HBM)
    out = pl.pallas_call(
        functools.partial(kernel, size_x, size_y),
        out_shape=jax.ShapeDtypeStruct((SIDE, SIDE, 2, 16, 4 * CO), BF16),
        in_specs=[hbm_spec] * 6,
        out_specs=pl.BlockSpec(memory_space=pl.ANY),
        scratch_shapes=[
            pltpu.SMEM((BRICKS, 27), jnp.int32),
            pltpu.SMEM((1, BRICKS), jnp.int32),
            pltpu.VMEM((ROWS, LANES), BF16),
            pltpu.VMEM((27, CH, CH), BF16),
            pltpu.VMEM((1, CH), F32),
            pltpu.VMEM((8, CH, CO), BF16),
            pltpu.SMEM((BRICKS, 27), jnp.int32),
            pltpu.VMEM((4, MESSAGE, LANES), BF16),
            pltpu.VMEM((4, MESSAGE, LANES), BF16),
            pltpu.VMEM((4, 16, LANES), BF16),
            pltpu.VMEM((T_SIZE, EDGE, LANES), F32),
            pltpu.VMEM((2, Y_SIZE, EDGE, LANES), F32),
            pltpu.VMEM((4, E_SIZE, EDGE, LANES), F32),
            pltpu.VMEM((BRICKS // 2, 3, 10, 2, 16, BAND), BF16),
            pltpu.VMEM((3, 3 * BAND, HALF), BF16),
            pltpu.VMEM((2 * HALF, 512), BF16),
            pltpu.VMEM((2, SIDE, EDGE, 128), F32),
            pltpu.VMEM((2, SIDE, 128, 128), BF16),
            pltpu.VMEM((2, BRICKS, 16, 256), BF16),
            pltpu.VMEM((2, SIDE, BRICKS, 16, 256), BF16),
            pltpu.VMEM((2, SIDE, SIDE, 2, 16, 256), BF16),
            pltpu.SemaphoreType.DMA((6,)),
            pltpu.SemaphoreType.DMA((8,)),
            pltpu.SemaphoreType.DMA((8,)),
            pltpu.SemaphoreType.DMA((2, SIDE)),
            pltpu.SemaphoreType.DMA((2, SIDE)),
            pltpu.SemaphoreType.DMA((2, 2, SIDE)),
            pltpu.SemaphoreType.DMA((2, 2, SIDE)),
            pltpu.SemaphoreType.DMA((2, SIDE)),
            pltpu.SemaphoreType.DMA((2, SIDE)),
            pltpu.SemaphoreType.DMA((2,)),
        ],
        compiler_params=pltpu.CompilerParams(
            collective_id=0, has_side_effects=True, vmem_limit_bytes=48 * 1024 * 1024
        ),
        name="brick_encoder",
    )(
        neighbour_ids,
        coarse_owner.reshape(1, BRICKS),
        features.reshape(ROWS, LANES),
        conv_weight,
        conv_bias.reshape(1, CH),
        down_weight,
    )
    return out.reshape(slots, 4, 4, 4 * CO)


def solution(mesh):
    in_specs = (
        P(("bx", "by"), None, None, None),
        P(("bx", "by"), None),
        P(),
        P(),
        P(),
        P(("bx", "by"), None),
    )
    out_specs = P(("bx", "by"), None, None, None)
    return jax.shard_map(shards, mesh=mesh, in_specs=in_specs, out_specs=out_specs, check_vma=False)
```

time: 29.7 us -> 33.1 us (1.11)
  Pallas kernels: 24.6 us -> 28.3 us
    pallas_call x1, Pallas kernels: 24.6 us -> 28.3 us  [shards(): pl.pallas_call(functools.partial(kernel, size_x, size_y), out_shape=jax.S...]
    unnamed x11 -> x12, local copies, waits for them, and re-layouts: 3.72 us -> 3.65 us
where the time goes in v2:
time: 33.1 us; the launch traced here: 32.9 us
  Pallas kernels  28.3 us (85%)
  local copies, waits for them, and re-layouts  4.57 us (14%)
    pallas_call x1, Pallas kernels, shards(): pl.pallas_call(functools.partial(kernel, size_x, size_y), out_shape=jax.S...  28.3 us
    unnamed x12, local copies, waits for them, and re-layouts  3.65 us
    reshape x1, local copies, waits for them, and re-layouts, shards(): return out.reshape(slots, 4, 4, 4 * CO)  0.92 us

profile of v2, /device:TPU:0, one launch (start us, length us, event | category | flops | bytes accessed | tf_op | source)
XLA Modules:
  0.0 32.9 jit_solution(14549555486682635277)
XLA Ops:
  0.0 0.0 copy-start.3
  0.0 0.0 copy-start.4
  0.0 0.0 copy-start.5
  0.0 0.7 %copy-done.3 = s32[8,27]{1,0:T(8,128)S(1)} copy-done((s32[8,27]{1,0:T(8,128)S(1)}, s32[8,27]{1,0:T(8,128)}, u32[]{:S(2)}) %copy-start.3) | copy-done | bytes 888
  0.7 0.0 copy-done.4
  0.7 0.0 copy-done.5
  0.7 0.0 copy-start
  0.7 1.0 %copy-done = bf16[8,8,8,512]{3,2,1,0:T(8,128)(2,1)S(1)} copy-done((bf16[8,8,8,512]{3,2,1,0:T(8,128)(2,1)S(1)}, bf16[8,8,8,512]{3,2,1,0:T(8,128)(2,1)}, u32[]{:S(2)}) %copy-start) | copy-done | bytes 524312
  1.7 0.0 copy-start.1
  1.7 1.0 %copy-done.1 = bf16[27,64,64]{2,1,0:T(8,128)(2,1)S(1)} copy-done((bf16[27,64,64]{2,1,0:T(8,128)(2,1)S(1)}, bf16[27,64,64]{2,1,0:T(8,128)(2,1)}, u32[]{:S(2)}) %copy-start.1) | copy-done | bytes 221208
  2.8 0.0 copy-start.2
  2.8 0.9 %copy-done.2 = bf16[8,64,128]{2,1,0:T(8,128)(2,1)S(1)} copy-done((bf16[8,64,128]{2,1,0:T(8,128)(2,1)S(1)}, bf16[8,64,128]{2,1,0:T(8,128)(2,1)}, u32[]{:S(2)}) %copy-start.2) | copy-done | bytes 131096
  3.7 28.3 %brick_encoder.1 = bf16[4,4,2,16,512]{4,3,2,1,0:T(8,128)(2,1)S(1)} custom-call(s32[8,27]{1,0:T(8,128)S(1)} %copy-done.3, s32[1,8]{1,0:T(1,128)S(1)} %bitcast.6, bf16[512,512]{1,0:T(8,128)(2,1)S(1)} %bitcast.5, bf16[27,64,64]{2,1,0:T(8,128)(2,1)S(1)} %copy-done.1, f32[1,64]{1,0:T(1,128)S(1)} %bitcast.7, bf16[8,64,128]{2,1,0:T(8,128)(2,1)S(1)} %copy-done.2), custom_call_target="tpu_custom_call" | custom-call | tf_op jit(solution)/shard_map/brick_encoder/pallas_call | solution.py:382
  31.9 0.9 %reshape.15 = bf16[32,4,4,512]{3,2,1,0:T(4,128)(2,1)} reshape(bf16[4,4,2,16,512]{4,3,2,1,0:T(8,128)(2,1)S(1)} %brick_encoder.1) | data formatting | bytes 1048576 | tf_op jit(solution)/shard_map/reshape | solution.py:432
Async XLA Ops:
  0.0 0.7 %copy-start.3 = (s32[8,27]{1,0:T(8,128)S(1)}, s32[8,27]{1,0:T(8,128)}, u32[]{:S(2)}) copy-start(s32[8,27]{1,0:T(8,128)} %ids_hbm.1) | copy-start | bytes 2596
  0.0 0.7 %copy-start.4 = (s32[8,1]{0,1:T(1,128)S(1)}, s32[8,1]{0,1:T(1,128)}, u32[]{:S(2)}) copy-start(s32[8,1]{0,1:T(1,128)} %param.11) | copy-start | bytes 100
  0.0 0.7 %copy-start.5 = (f32[64]{0:T(128)S(1)}, f32[64]{0:T(128)}, u32[]{:S(2)}) copy-start(f32[64]{0:T(128)} %param.9) | copy-start | bytes 772
  0.7 1.0 %copy-start = (bf16[8,8,8,512]{3,2,1,0:T(8,128)(2,1)S(1)}, bf16[8,8,8,512]{3,2,1,0:T(8,128)(2,1)}, u32[]{:S(2)}) copy-start(bf16[8,8,8,512]{3,2,1,0:T(8,128)(2,1)} %param.6) | copy-start | bytes 1572868
  1.7 1.0 %copy-start.1 = (bf16[27,64,64]{2,1,0:T(8,128)(2,1)S(1)}, bf16[27,64,64]{2,1,0:T(8,128)(2,1)}, u32[]{:S(2)}) copy-start(bf16[27,64,64]{2,1,0:T(8,128)(2,1)} %conv_hbm.1) | copy-start | bytes 663556
  2.8 0.9 %copy-start.2 = (bf16[8,64,128]{2,1,0:T(8,128)(2,1)S(1)}, bf16[8,64,128]{2,1,0:T(8,128)(2,1)}, u32[]{:S(2)}) copy-start(bf16[8,64,128]{2,1,0:T(8,128)(2,1)} %down_hbm.1) | copy-start | bytes 393220

commit v3 on v1

v3 whole, which is shorter than its diff:
```python
import functools

import jax
import jax.numpy as jnp
from jax import lax
from jax.experimental import pallas as pl
from jax.experimental.pallas import tpu as pltpu
from jax.sharding import PartitionSpec as P

MESH = pl.DeviceIdType.MESH
F32 = jnp.float32
BF16 = jnp.bfloat16

EDGE = 8
BRICKS = 8
CH = 64
CO = 128
LANES = EDGE * CH
ROWS = BRICKS * EDGE * EDGE
HALF = 4 * CH
BAND = 6 * CH
FACE = BRICKS * EDGE

T_FACE = BRICKS * EDGE
T_ZERO = T_FACE + 2 * BRICKS
T_SIZE = T_ZERO + EDGE
Y_ZERO = 2 * BRICKS
Y_SIZE = Y_ZERO + 1
E_ZERO = 4 * BRICKS
E_SIZE = E_ZERO + 1

STEPS = (-1, 0, 1)
CHUNK = 1
CHUNKS = EDGE // 2 // CHUNK
SENT = 8 * CHUNK
HALO = [(1, 0), (-1, 0), (0, 1), (0, -1), (1, 1), (1, -1), (-1, 1), (-1, -1)]


def iota(shape, dim):
    return lax.broadcasted_iota(jnp.int32, shape, dim)


def picked_rows():
    targets = []
    inner = iota((FACE, 128), 0)
    for first in (56, 0):
        targets.append((inner >> 3) * 64 + first + (inner & 7))
    for first in (7, 0):
        targets.append(inner * 8 + first)
    inner = iota((4 * BRICKS, 128), 0)
    corner = inner >> 3
    targets.append(
        (inner & 7) * 64 + jnp.where(corner < 2, 56, 0) + jnp.where(corner & 1 == 0, 7, 0)
    )
    target = jnp.concatenate(targets, 0)
    target = target - iota(target.shape, 1)
    blocks = [(target == 128 * k).astype(F32) for k in range(ROWS // 128)]
    return jnp.concatenate(blocks, 1).astype(BF16)


def repeat_rows(target, corner, first, rows, start=0, step=1):
    for k in range(BRICKS):
        row = start + step * k
        target[corner, first + k] = jnp.broadcast_to(rows[row : row + 1], (EDGE, LANES))


def kernel(
    size_x, size_y,
    ids_hbm, owner_hbm, feat_hbm, conv_hbm, bias_hbm, down_hbm,
    out_ref,
    ids, owner, feat, conv, bias, down,
    index, face_send, edge_send, face_recv, edge_recv, table, ytab, etab,
    stack, band, down_both, place, stage,
    load_sem, halo_send, halo_recv, out_send, out_recv, own_sem,
):
    i = lax.axis_index("bx")
    j = lax.axis_index("by")

    loads = [
        pltpu.make_async_copy(source, target, load_sem.at[k])
        for k, (source, target) in enumerate(
            [
                (feat_hbm, feat),
                (conv_hbm, conv),
                (ids_hbm, ids),
                (owner_hbm, owner),
                (bias_hbm, bias),
                (down_hbm, down),
            ]
        )
    ]
    for load in loads:
        load.start()

    def beside(step_x, step_y):
        return (lax.rem(i + step_x + size_x, size_x), lax.rem(j + step_y + size_y, size_y))

    barrier = pltpu.get_barrier_semaphore()
    greeted = [beside(sx, sy) for sx, sy in HALO if sx]
    greeted += [beside(0, d) for d in range(1, size_y)]
    for device in greeted:
        pl.semaphore_signal(barrier, inc=1, device_id=device, device_id_type=MESH)

    def remote(source, target, send_sem, recv_sem, device):
        copy = pltpu.make_async_remote_copy(
            src_ref=source,
            dst_ref=target,
            send_sem=send_sem,
            recv_sem=recv_sem,
            device_id=device,
            device_id_type=MESH,
        )
        copy.start()
        return copy

    pick = picked_rows()
    loads[0].wait()
    picked = jnp.dot(pick, feat[...], preferred_element_type=F32)
    for k in range(4):
        face_send[k] = picked[k * FACE : (k + 1) * FACE].astype(BF16)
        first = 4 * FACE + k * BRICKS
        edge = picked[first : first + BRICKS]
        edge_send[k] = jnp.concatenate([edge[:, 0:256], edge[:, 256:512]], 0).astype(BF16)

    pl.semaphore_wait(barrier, len(greeted))
    copies = []
    for k, (sx, sy) in enumerate(HALO):
        if k < 4:
            source, target = face_send.at[k], face_recv.at[k]
        else:
            source, target = edge_send.at[k - 4], edge_recv.at[k - 4]
        copies.append(
            remote(source, target, halo_send.at[k], halo_recv.at[k], beside(sx, sy))
        )

    table[0:T_FACE] = feat[...].astype(F32).reshape(T_FACE, EDGE, LANES)
    table[T_ZERO:T_SIZE] = jnp.zeros((EDGE, EDGE, LANES), F32)
    for k in range(2):
        ytab[k, 0:BRICKS] = picked[(2 + k) * FACE : (3 + k) * FACE].reshape(BRICKS, EDGE, LANES)
        ytab[k, Y_ZERO] = jnp.zeros((EDGE, LANES), F32)
    for k in range(4):
        repeat_rows(etab, k, 0, picked, 4 * FACE + k * BRICKS)
        etab[k, E_ZERO] = jnp.zeros((EDGE, LANES), F32)

    loads[2].wait()
    for g in range(BRICKS):
        for tap in range(27):
            sx, sy = tap // 9 - 1, tap // 3 % 3 - 1
            value = ids[g, tap]
            brick = value & 7
            far_x = jnp.where(value >> 3 >> 4 == i, 0, 1)
            far_y = jnp.where((value >> 3) & 15 == j, 0, 1)
            if sx == 0 and sy == 0:
                row, zero = brick * EDGE, T_ZERO
            elif sy == 0:
                edge_x, side = (7, 0) if sx < 0 else (0, 1)
                row = jnp.where(far_x == 0, brick * EDGE + edge_x, T_FACE + side * BRICKS + brick)
                zero = T_ZERO
            elif sx == 0:
                row, zero = far_y * BRICKS + brick, Y_ZERO
            else:
                row, zero = far_x * 16 + far_y * 8 + brick, E_ZERO
            index[g, tap] = jnp.where(value >= 0, row, zero)

    loads[1].wait()
    empty = jnp.zeros((CH, CH), BF16)
    blank = jnp.zeros((CH, 2 * CH), BF16)
    for ty in range(3):
        for tx in range(3):
            w = [conv[tx * 9 + ty * 3 + tz] * jnp.array(0.5, BF16) for tz in range(3)]
            pairs = {
                -1: jnp.concatenate([w[0], empty], 1),
                0: jnp.concatenate([w[1], w[0]], 1),
                1: jnp.concatenate([w[2], w[1]], 1),
                2: jnp.concatenate([empty, w[2]], 1),
            }
            for place_in, depth_in in enumerate((0, 1, 2, 3, 4, -1)):
                for q in range(2):
                    first = tx * BAND + place_in * CH
                    band[ty, first : first + CH, q * 128 : (q + 1) * 128] = pairs.get(
                        depth_in - 2 * q, blank
                    )
    loads[5].wait()
    for a in range(2):
        for b in range(2):
            for k in range(2):
                first = (a * 2 + k) * CH
                down_both[first : first + CH, b * CO : (b + 1) * CO] = down[a * 4 + b * 2 + k]

    loads[3].wait()
    owners = [owner[0, g] for g in range(BRICKS)]
    row, col = iota((4 * CHUNK, 64 * CHUNK), 0), iota((4 * CHUNK, 64 * CHUNK), 1)
    slot_of = jnp.zeros((4 * CHUNK, 64 * CHUNK), jnp.int32)
    for g in range(BRICKS):
        rank = jnp.int32(0)
        for earlier in range(g):
            rank = rank + jnp.where(owners[earlier] == owners[g], 1, 0)
        slot_of = jnp.where((col >> 3) & 7 == g, owners[g] * 2 + rank, slot_of)
    slot_of = jnp.where((col >> 6 == row >> 2) & (col & 7 == (row & 3) * 2), slot_of, -1)
    rows = 8 if CHUNK == 1 else 4 * CHUNK
    slot_of = jnp.concatenate([slot_of] * (rows // (4 * CHUNK)), 0)
    row = iota(slot_of.shape, 0) >> (2 + CHUNK - 1)
    for s in range(0, 2 * size_y, rows // (4 * CHUNK)):
        block = (slot_of == row + s).astype(F32) if CHUNK == 1 else (slot_of == s).astype(F32)
        first = s * 4 * CHUNK
        place[first : first + rows] = block

    loads[4].wait()
    for copy in copies:
        copy.wait()
    for k in range(2):
        over_x = face_recv[k].astype(F32)
        over_y = face_recv[2 + k].astype(F32)
        first = T_FACE + k * BRICKS
        table[first : first + BRICKS] = over_x.reshape(BRICKS, EDGE, LANES)
        ytab[k, BRICKS : 2 * BRICKS] = over_y.reshape(BRICKS, EDGE, LANES)
        for side in range(2):
            at = 0 if side else 7
            repeat_rows(etab, side * 2 + k, 8, over_y, at, EDGE)
            repeat_rows(etab, k * 2 + side, 16, over_x, at, EDGE)
            edge = edge_recv[k * 2 + side].astype(F32)
            edge = jnp.concatenate([edge[0:8], edge[8:16]], 1)
            repeat_rows(etab, k * 2 + side, 24, edge)

    low = iota((EDGE, 128), 1) < CH
    last_row = iota((EDGE, BAND), 0) == 7
    first_row = iota((EDGE, BAND), 0) == 0

    def halves(read, centre, minus, plus):
        c = read(centre, 0, LANES)
        m = read(minus, LANES - 128, LANES)
        p = read(plus, 0, 128)
        e0 = jnp.where(low, c[:, 256:384], m)
        e1 = jnp.where(low, p, c[:, 128:256])
        return (
            jnp.concatenate([c[:, 0:256], e0], 1),
            jnp.concatenate([c[:, 256:512], e1], 1),
        )

    def one_slab(g, x):
        sx = -1 if x < 0 else (1 if x > 7 else 0)
        shift = x if sx == 0 else 0
        result = []
        for sy in STEPS:
            tap = (sx + 1) * 9 + (sy + 1) * 3
            if sy == 0:
                def read(row, low_lane, high_lane):
                    return table[row + shift, :, low_lane:high_lane]
            elif sx == 0:
                def read(row, low_lane, high_lane, side=(sy + 1) // 2):
                    lines = ytab[side, row, :, low_lane:high_lane]
                    return pltpu.roll(lines, (7 - x if side == 0 else 0 - x) & 7, 0)
            else:
                def read(row, low_lane, high_lane, corner=(sx + 1) // 2 * 2 + (sy + 1) // 2):
                    return etab[corner, row, :, low_lane:high_lane]
            result.append(halves(read, index[g, tap + 1], index[g, tap], index[g, tap + 2]))
        before, same, after = result
        return [
            [jnp.where(last_row, before[h], same[h]), same[h], jnp.where(first_row, after[h], same[h])]
            for h in range(2)
        ]

    def gather(slabs):
        for x in slabs:
            for pair in range(BRICKS // 2):
                even = one_slab(pair * 2, x)
                odd = one_slab(pair * 2 + 1, x)
                for h in range(2):
                    for ty in range(3):
                        both = jnp.concatenate([even[h][ty], odd[h][ty]], 0)
                        stack[ty, x + 1, h, pair * 16 : pair * 16 + 16] = both.astype(BF16)

    def out_copy(chunk, d):
        dest = lax.rem(j + d, size_y)
        return pltpu.make_async_remote_copy(
            src_ref=stage.at[chunk, dest],
            dst_ref=out_ref.at[j, chunk],
            send_sem=out_send.at[chunk, d],
            recv_sem=out_recv.at[chunk, d],
            device_id=(i, dest),
            device_id_type=MESH,
        )

    def own_copy(chunk):
        return pltpu.make_async_copy(stage.at[chunk, j], out_ref.at[j, chunk], own_sem.at[chunk])

    bias_row = jnp.concatenate([bias[...] * 0.5] * 4, 1)
    slabs = 2 * CHUNK
    size = slabs * 2 * FACE
    gather([-1, 0])
    for chunk in range(CHUNKS):
        base = chunk * slabs
        gather(range(base + 1, base + slabs + 1))
        total = None
        for ty in range(3):
            window = jnp.concatenate(
                [
                    stack[ty, base + tx : base + tx + slabs].reshape(size, BAND)
                    for tx in range(3)
                ],
                1,
            )
            part = jnp.dot(window, band[ty], preferred_element_type=F32)
            if ty != 1:
                part = pltpu.roll(part.reshape(size // 8, 8, HALF), 1 if ty == 0 else 7, 1)
                part = part.reshape(size, HALF)
            total = part if total is None else total + part
        half_v = total + bias_row
        own = stack[1, base + 1 : base + 1 + slabs, :, :, 0:HALF].reshape(size, HALF)
        hidden = own.astype(F32) + (half_v + half_v * jnp.tanh(half_v))
        hidden = hidden.astype(BF16).reshape(CHUNK, 2, 2 * FACE, HALF)
        lhs = jnp.concatenate(
            [
                jnp.concatenate([hidden[:, a, :, k * 128 : (k + 1) * 128] for a in range(2)], 2)
                for k in range(2)
            ],
            0,
        ).reshape(2 * CHUNK * 2 * FACE, 256)
        coarse = jnp.dot(lhs, down_both[...], preferred_element_type=F32)
        odd = pltpu.roll(coarse[:, CO:].reshape(-1, 8, CO), 7, 1).reshape(-1, CO)
        coarse = (coarse[:, :CO] + odd).astype(BF16).reshape(2, CHUNK, 2, FACE, CO)
        coarse = jnp.concatenate(
            [coarse[k, :, h] for h in range(2) for k in range(2)], 2
        ).reshape(CHUNK * FACE, 4 * CO)
        placed = jnp.dot(place[...].astype(BF16), coarse, preferred_element_type=F32)
        stage[chunk] = placed.reshape(size_y, SENT, 4 * CO).astype(BF16)
        for d in range(1, size_y):
            out_copy(chunk, d).start()
        own_copy(chunk).start()
    for chunk in range(CHUNKS):
        for d in range(1, size_y):
            out_copy(chunk, d).wait()
        own_copy(chunk).wait()


def shards(features, neighbour_ids, conv_weight, conv_bias, down_weight, coarse_owner):
    size_x = lax.axis_size("bx")
    size_y = lax.axis_size("by")
    slots = 2 * size_y
    hbm_spec = pl.BlockSpec(memory_space=pltpu.HBM)
    out = pl.pallas_call(
        functools.partial(kernel, size_x, size_y),
        out_shape=jax.ShapeDtypeStruct((size_y, CHUNKS, SENT, 4 * CO), BF16),
        in_specs=[hbm_spec] * 6,
        out_specs=pl.BlockSpec(memory_space=pl.ANY),
        scratch_shapes=[
            pltpu.SMEM((BRICKS, 27), jnp.int32),
            pltpu.SMEM((1, BRICKS), jnp.int32),
            pltpu.VMEM((ROWS, LANES), BF16),
            pltpu.VMEM((27, CH, CH), BF16),
            pltpu.VMEM((1, CH), F32),
            pltpu.VMEM((8, CH, CO), BF16),
            pltpu.SMEM((BRICKS, 27), jnp.int32),
            pltpu.VMEM((4, FACE, LANES), BF16),
            pltpu.VMEM((4, 16, 256), BF16),
            pltpu.VMEM((4, FACE, LANES), BF16),
            pltpu.VMEM((4, 16, 256), BF16),
            pltpu.VMEM((T_SIZE, EDGE, LANES), F32),
            pltpu.VMEM((2, Y_SIZE, EDGE, LANES), F32),
            pltpu.VMEM((4, E_SIZE, EDGE, LANES), F32),
            pltpu.VMEM((3, 10, 2, FACE, BAND), BF16),
            pltpu.VMEM((3, 3 * BAND, HALF), BF16),
            pltpu.VMEM((256, 2 * CO), BF16),
            pltpu.VMEM((slots * 4 * CHUNK, FACE * CHUNK), F32),
            pltpu.VMEM((CHUNKS, size_y, SENT, 4 * CO), BF16),
            pltpu.SemaphoreType.DMA((6,)),
            pltpu.SemaphoreType.DMA((8,)),
            pltpu.SemaphoreType.DMA((8,)),
            pltpu.SemaphoreType.DMA((CHUNKS, size_y)),
            pltpu.SemaphoreType.DMA((CHUNKS, size_y)),
            pltpu.SemaphoreType.DMA((CHUNKS,)),
        ],
        compiler_params=pltpu.CompilerParams(
            collective_id=0, has_side_effects=True, vmem_limit_bytes=63 * 1024 * 1024
        ),
        name="brick_encoder",
    )(
        neighbour_ids,
        coarse_owner.reshape(1, BRICKS),
        features.reshape(ROWS, LANES),
        conv_weight,
        conv_bias.reshape(1, CH),
        down_weight,
    )
    out = out.reshape(size_y, CHUNKS, 2, CHUNK, 4, 4 * CO)
    return out.transpose(0, 2, 1, 3, 4, 5).reshape(slots, 4, 4, 4 * CO)


def solution(mesh):
    in_specs = (
        P(("bx", "by"), None, None, None),
        P(("bx", "by"), None),
        P(),
        P(),
        P(),
        P(("bx", "by"), None),
    )
    out_specs = P(("bx", "by"), None, None, None)
    return jax.shard_map(shards, mesh=mesh, in_specs=in_specs, out_specs=out_specs, check_vma=False)
```

time: 29.7 us -> 27 us (0.909)
  local copies, waits for them, and re-layouts: 4.64 us -> 2.23 us
    unnamed x11 -> x0, local copies, waits for them, and re-layouts: 3.72 us -> none
    transpose x0 -> x1, local copies, waits for them, and re-layouts: none -> 1.06 us  [shards(): return out.transpose(0, 2, 1, 3, 4, 5).reshape(slots, 4, 4, 4 * CO)]
where the time goes in v3:
time: 27 us; the launch traced here: 26.7 us
  Pallas kernels  24.5 us (91%)
  local copies, waits for them, and re-layouts  2.23 us (8%)
    pallas_call x1, Pallas kernels, shards(): pl.pallas_call(functools.partial(kernel, size_x, size_y), out_shape=jax.S...  24.5 us
    reshape x1, local copies, waits for them, and re-layouts, shards(): out = out.reshape(size_y, CHUNKS, 2, CHUNK, 4, 4 * CO)  1.17 us
    transpose x1, local copies, waits for them, and re-layouts, shards(): return out.transpose(0, 2, 1, 3, 4, 5).reshape(slots, 4, 4, 4 * CO)  1.06 us

profile of v3, /device:TPU:0, one launch (start us, length us, event | category | flops | bytes accessed | tf_op | source)
XLA Modules:
  0.0 26.7 jit_solution(11975501211455059995)
XLA Ops:
  0.0 24.5 %brick_encoder.1 = bf16[16,4,8,512]{3,2,1,0:T(8,128)(2,1)} custom-call(s32[8,27]{1,0:T(8,128)} %ids_hbm.1, s32[1,8]{1,0:T(1,128)} %bitcast.9, bf16[512,512]{1,0:T(8,128)(2,1)} %bitcast.8, bf16[27,64,64]{2,1,0:T(8,128)(2,1)} %conv_hbm.1, f32[1,64]{1,0:T(1,128)} %bitcast.10, bf16[8,64,128]{2,1,0:T(8,128)(2,1)} %down_hbm.1), custom_call_target="tpu_custom_call" | custom-call | tf_op jit(solution)/shard_map/brick_encoder/pallas_call | solution.py:341
  24.5 1.2 %reshape.18 = bf16[16,4,2,1,4,512]{5,4,2,1,0,3:T(4,128)(2,1)S(1)} reshape(bf16[16,4,8,512]{3,2,1,0:T(8,128)(2,1)} %brick_encoder.1) | data formatting | bytes 1048576 | tf_op jit(solution)/shard_map/reshape | solution.py:385
  25.6 1.1 %copy.7 = bf16[16,2,4,1,4,512]{5,4,2,1,0,3:T(4,128)(2,1)} copy(bf16[16,2,4,1,4,512]{5,4,1,2,0,3:T(4,128)(2,1)S(1)} %bitcast.7) | data formatting | bytes 1048576 | tf_op jit(solution)/shard_map/transpose | solution.py:386

commit v4 on v3

--- a/solution.py
+++ b/solution.py
@@ -30,9 +30,9 @@
 E_SIZE = E_ZERO + 1
 
 STEPS = (-1, 0, 1)
-CHUNK = 1
+CHUNK = 2
 CHUNKS = EDGE // 2 // CHUNK
-SENT = 8 * CHUNK
+SIDE = 4
 HALO = [(1, 0), (-1, 0), (0, 1), (0, -1), (1, 1), (1, -1), (-1, 1), (-1, -1)]
 
 
@@ -71,10 +71,11 @@
     ids, owner, feat, conv, bias, down,
     index, face_send, edge_send, face_recv, edge_recv, table, ytab, etab,
     stack, band, down_both, place, stage,
-    load_sem, halo_send, halo_recv, out_send, out_recv, own_sem,
+    load_sem, halo_send, halo_recv, out_send, out_recv, own_sem, known_sem,
 ):
     i = lax.axis_index("bx")
     j = lax.axis_index("by")
+    z, y = j // SIDE, lax.rem(j, SIDE)
 
     loads = [
         pltpu.make_async_copy(source, target, load_sem.at[k])
@@ -92,26 +93,32 @@
     for load in loads:
         load.start()
 
-    def beside(step_x, step_y):
-        return (lax.rem(i + step_x + size_x, size_x), lax.rem(j + step_y + size_y, size_y))
+    def inside(step_x, step_y):
+        x_in = (i + step_x >= 0) & (i + step_x < size_x)
+        return x_in & (j + step_y >= 0) & (j + step_y < size_y)
+
+    def partner(step_z, step_y):
+        return lax.rem(z + step_z, SIDE) * SIDE + lax.rem(y + step_y, SIDE)
+
+    straight = [(0, d) for d in range(1, SIDE)] + [(d, 0) for d in range(1, SIDE)]
+    turning = [(a, b) for a in range(1, SIDE) for b in range(1, SIDE)]
 
     barrier = pltpu.get_barrier_semaphore()
-    greeted = [beside(sx, sy) for sx, sy in HALO if sx]
-    greeted += [beside(0, d) for d in range(1, size_y)]
-    for device in greeted:
-        pl.semaphore_signal(barrier, inc=1, device_id=device, device_id_type=MESH)
-
-    def remote(source, target, send_sem, recv_sem, device):
-        copy = pltpu.make_async_remote_copy(
-            src_ref=source,
-            dst_ref=target,
-            send_sem=send_sem,
-            recv_sem=recv_sem,
-            device_id=device,
-            device_id_type=MESH,
-        )
-        copy.start()
-        return copy
+    greetings = jnp.int32(len(straight))
+    for step_x, step_y in HALO:
+        here = inside(step_x, step_y)
+        greetings = greetings + jnp.where(here, 1, 0)
+
+        @pl.when(here)
+        def _(step_x=step_x, step_y=step_y):
+            pl.semaphore_signal(
+                barrier, inc=1, device_id=(i + step_x, j + step_y), device_id_type=MESH
+            )
+
+    for steps in straight:
+        pl.semaphore_signal(
+            barrier, inc=1, device_id=(i, partner(*steps)), device_id_type=MESH
+        )
 
     pick = picked_rows()
     loads[0].wait()
@@ -122,15 +129,26 @@
         edge = picked[first : first + BRICKS]
         edge_send[k] = jnp.concatenate([edge[:, 0:256], edge[:, 256:512]], 0).astype(BF16)
 
-    pl.semaphore_wait(barrier, len(greeted))
+    pl.semaphore_wait(barrier, greetings)
     copies = []
-    for k, (sx, sy) in enumerate(HALO):
+    for k, (step_x, step_y) in enumerate(HALO):
         if k < 4:
             source, target = face_send.at[k], face_recv.at[k]
         else:
             source, target = edge_send.at[k - 4], edge_recv.at[k - 4]
-        copies.append(
-            remote(source, target, halo_send.at[k], halo_recv.at[k], beside(sx, sy))
+        copy = pltpu.make_async_remote_copy(
+            src_ref=source,
+            dst_ref=target,
+            send_sem=halo_send.at[k],
+            recv_sem=halo_recv.at[k],
+            device_id=(i + step_x, j + step_y),
+            device_id_type=MESH,
+        )
+        copies.append((copy, inside(step_x, step_y), inside(-step_x, -step_y)))
+        pl.when(copies[-1][1])(copy.start)
+    for d in range(1, SIDE):
+        pl.semaphore_signal(
+            known_sem, inc=1, device_id=(i, partner(0, d)), device_id_type=MESH
         )
 
     table[0:T_FACE] = feat[...].astype(F32).reshape(T_FACE, EDGE, LANES)
@@ -189,25 +207,21 @@
 
     loads[3].wait()
     owners = [owner[0, g] for g in range(BRICKS)]
-    row, col = iota((4 * CHUNK, 64 * CHUNK), 0), iota((4 * CHUNK, 64 * CHUNK), 1)
-    slot_of = jnp.zeros((4 * CHUNK, 64 * CHUNK), jnp.int32)
+    row, col = iota((8 * CHUNK, FACE * CHUNK), 0), iota((8 * CHUNK, FACE * CHUNK), 1)
+    slot_of = jnp.zeros((8 * CHUNK, FACE * CHUNK), jnp.int32)
     for g in range(BRICKS):
         rank = jnp.int32(0)
         for earlier in range(g):
             rank = rank + jnp.where(owners[earlier] == owners[g], 1, 0)
         slot_of = jnp.where((col >> 3) & 7 == g, owners[g] * 2 + rank, slot_of)
-    slot_of = jnp.where((col >> 6 == row >> 2) & (col & 7 == (row & 3) * 2), slot_of, -1)
-    rows = 8 if CHUNK == 1 else 4 * CHUNK
-    slot_of = jnp.concatenate([slot_of] * (rows // (4 * CHUNK)), 0)
-    row = iota(slot_of.shape, 0) >> (2 + CHUNK - 1)
-    for s in range(0, 2 * size_y, rows // (4 * CHUNK)):
-        block = (slot_of == row + s).astype(F32) if CHUNK == 1 else (slot_of == s).astype(F32)
-        first = s * 4 * CHUNK
-        place[first : first + rows] = block
+    slot_of = jnp.where((col >> 6 == row >> 3) & (col & 7 == (row & 7) * 2), slot_of, -1)
+    blocks = [(slot_of == s).astype(F32) for s in range(2 * size_y)]
+    place[...] = jnp.concatenate(blocks, 0).astype(BF16)
 
     loads[4].wait()
-    for copy in copies:
-        copy.wait()
+    for copy, sent, received in copies:
+        pl.when(sent)(copy.wait_send)
+        pl.when(received)(copy.wait_recv)
     for k in range(2):
         over_x = face_recv[k].astype(F32)
         over_y = face_recv[2 + k].astype(F32)
@@ -270,19 +284,23 @@
                         both = jnp.concatenate([even[h][ty], odd[h][ty]], 0)
                         stack[ty, x + 1, h, pair * 16 : pair * 16 + 16] = both.astype(BF16)
 
-    def out_copy(chunk, d):
-        dest = lax.rem(j + d, size_y)
+    def out_copy(chunk, steps):
+        dest = partner(*steps)
         return pltpu.make_async_remote_copy(
-            src_ref=stage.at[chunk, dest],
-            dst_ref=out_ref.at[j, chunk],
-            send_sem=out_send.at[chunk, d],
-            recv_sem=out_recv.at[chunk, d],
+            src_ref=stage.at[chunk, pl.ds(dest * 2, 2)],
+            dst_ref=out_ref.at[pl.ds(j * 2, 2), pl.ds(chunk * CHUNK, CHUNK)],
+            send_sem=out_send.at[chunk, steps[0] * SIDE + steps[1]],
+            recv_sem=out_recv.at[chunk, steps[0] * SIDE + steps[1]],
             device_id=(i, dest),
             device_id_type=MESH,
         )
 
     def own_copy(chunk):
-        return pltpu.make_async_copy(stage.at[chunk, j], out_ref.at[j, chunk], own_sem.at[chunk])
+        return pltpu.make_async_copy(
+            stage.at[chunk, pl.ds(j * 2, 2)],
+            out_ref.at[pl.ds(j * 2, 2), pl.ds(chunk * CHUNK, CHUNK)],
+            own_sem.at[chunk],
+        )
 
     bias_row = jnp.concatenate([bias[...] * 0.5] * 4, 1)
     slabs = 2 * CHUNK
@@ -322,14 +340,19 @@
         coarse = jnp.concatenate(
             [coarse[k, :, h] for h in range(2) for k in range(2)], 2
         ).reshape(CHUNK * FACE, 4 * CO)
-        placed = jnp.dot(place[...].astype(BF16), coarse, preferred_element_type=F32)
-        stage[chunk] = placed.reshape(size_y, SENT, 4 * CO).astype(BF16)
-        for d in range(1, size_y):
-            out_copy(chunk, d).start()
+        placed = jnp.dot(place[...], coarse, preferred_element_type=F32)
+        placed = placed.reshape(2 * size_y, CHUNK, 8, 4 * CO)[:, :, 0:4]
+        stage[chunk] = placed.astype(BF16)
+        for steps in straight:
+            out_copy(chunk, steps).start()
+        if chunk == 0:
+            pl.semaphore_wait(known_sem, SIDE - 1)
+        for steps in turning:
+            out_copy(chunk, steps).start()
         own_copy(chunk).start()
     for chunk in range(CHUNKS):
-        for d in range(1, size_y):
-            out_copy(chunk, d).wait()
+        for steps in straight + turning:
+            out_copy(chunk, steps).wait()
         own_copy(chunk).wait()
 
 
@@ -338,9 +361,9 @@
     size_y = lax.axis_size("by")
     slots = 2 * size_y
     hbm_spec = pl.BlockSpec(memory_space=pltpu.HBM)
-    out = pl.pallas_call(
+    return pl.pallas_call(
         functools.partial(kernel, size_x, size_y),
-        out_shape=jax.ShapeDtypeStruct((size_y, CHUNKS, SENT, 4 * CO), BF16),
+        out_shape=jax.ShapeDtypeStruct((slots, 4, 4, 4 * CO), BF16),
         in_specs=[hbm_spec] * 6,
         out_specs=pl.BlockSpec(memory_space=pl.ANY),
         scratch_shapes=[
@@ -361,14 +384,15 @@
             pltpu.VMEM((3, 10, 2, FACE, BAND), BF16),
             pltpu.VMEM((3, 3 * BAND, HALF), BF16),
             pltpu.VMEM((256, 2 * CO), BF16),
-            pltpu.VMEM((slots * 4 * CHUNK, FACE * CHUNK), F32),
-            pltpu.VMEM((CHUNKS, size_y, SENT, 4 * CO), BF16),
+            pltpu.VMEM((slots * 8 * CHUNK, FACE * CHUNK), BF16),
+            pltpu.VMEM((CHUNKS, slots, CHUNK, 4, 4 * CO), BF16),
             pltpu.SemaphoreType.DMA((6,)),
             pltpu.SemaphoreType.DMA((8,)),
             pltpu.SemaphoreType.DMA((8,)),
             pltpu.SemaphoreType.DMA((CHUNKS, size_y)),
             pltpu.SemaphoreType.DMA((CHUNKS, size_y)),
             pltpu.SemaphoreType.DMA((CHUNKS,)),
+            pltpu.SemaphoreType.REGULAR,
         ],
         compiler_params=pltpu.CompilerParams(
             collective_id=0, has_side_effects=True, vmem_limit_bytes=63 * 1024 * 1024
@@ -382,8 +406,6 @@
         conv_bias.reshape(1, CH),
         down_weight,
     )
-    out = out.reshape(size_y, CHUNKS, 2, CHUNK, 4, 4 * CO)
-    return out.transpose(0, 2, 1, 3, 4, 5).reshape(slots, 4, 4, 4 * CO)
 
 
 def solution(mesh):

time: 27 us -> 25.5 us (0.944)
  Pallas kernels: 24.5 us -> 23 us
    unnamed x0 -> x1, local copies, waits for them, and re-layouts: none -> 2.06 us
    pallas_call x1, Pallas kernels: 24.5 us -> 23 us  [shards(): pl.pallas_call(functools.partial(kernel, size_x, size_y), out_shape=jax.S...]
    reshape x1 -> x0, local copies, waits for them, and re-layouts: 1.17 us -> none  [shards(): out = out.reshape(size_y, CHUNKS, 2, CHUNK, 4, 4 * CO)]
    transpose x1 -> x0, local copies, waits for them, and re-layouts: 1.06 us -> none  [shards(): return out.transpose(0, 2, 1, 3, 4, 5).reshape(slots, 4, 4, 4 * CO)]
where the time goes in v4:
time: 25.5 us; the launch traced here: 25.1 us
  Pallas kernels  23 us (90%)
  local copies, waits for them, and re-layouts  2.06 us (8%)
    pallas_call x1, Pallas kernels, shards(): pl.pallas_call(functools.partial(kernel, size_x, size_y), out_shape=jax.S...  23 us
    unnamed x1, local copies, waits for them, and re-layouts  2.06 us

profile of v4, /device:TPU:0, one launch (start us, length us, event | category | flops | bytes accessed | tf_op | source)
XLA Modules:
  0.0 25.1 jit_solution(535193524738833985)
XLA Ops:
  0.0 23.0 %brick_encoder.1 = bf16[32,4,4,512]{3,2,1,0:T(4,128)(2,1)} custom-call(s32[8,27]{1,0:T(8,128)} %ids_hbm.1, s32[1,8]{1,0:T(1,128)} %bitcast.4, bf16[512,512]{1,0:T(8,128)(2,1)} %bitcast.3, bf16[27,64,64]{2,1,0:T(8,128)(2,1)} %conv_hbm.1, f32[1,64]{1,0:T(1,128)} %bitcast.5, bf16[8,64,128]{2,1,0:T(8,128)(2,1)} %down_hbm.1), custom_call_target="tpu_custom_call" | custom-call | tf_op jit(solution)/shard_map/brick_encoder/pallas_call | solution.py:364
  23.0 2.1 %copy.8 = bf16[32,4,4,512]{3,2,1,0:T(4,128)(2,1)} copy(bf16[32,4,4,512]{3,2,1,0:T(4,128)(2,1)} %brick_encoder.1) | data formatting | bytes 1048576

commit v5 on v4

--- a/solution.py
+++ b/solution.py
@@ -33,6 +33,7 @@
 CHUNK = 2
 CHUNKS = EDGE // 2 // CHUNK
 SIDE = 4
+PARTS = 4
 HALO = [(1, 0), (-1, 0), (0, 1), (0, -1), (1, 1), (1, -1), (-1, 1), (-1, -1)]
 
 
@@ -104,6 +105,10 @@
     turning = [(a, b) for a in range(1, SIDE) for b in range(1, SIDE)]
 
     barrier = pltpu.get_barrier_semaphore()
+    for steps in straight:
+        pl.semaphore_signal(
+            barrier, inc=1, device_id=(i, partner(*steps)), device_id_type=MESH
+        )
     greetings = jnp.int32(len(straight))
     for step_x, step_y in HALO:
         here = inside(step_x, step_y)
@@ -114,11 +119,6 @@
             pl.semaphore_signal(
                 barrier, inc=1, device_id=(i + step_x, j + step_y), device_id_type=MESH
             )
-
-    for steps in straight:
-        pl.semaphore_signal(
-            barrier, inc=1, device_id=(i, partner(*steps)), device_id_type=MESH
-        )
 
     pick = picked_rows()
     loads[0].wait()
@@ -145,7 +145,8 @@
             device_id_type=MESH,
         )
         copies.append((copy, inside(step_x, step_y), inside(-step_x, -step_y)))
-        pl.when(copies[-1][1])(copy.start)
+    for copy, sent, received in copies[4:] + copies[2:4] + copies[:2]:
+        pl.when(sent)(copy.start)
     for d in range(1, SIDE):
         pl.semaphore_signal(
             known_sem, inc=1, device_id=(i, partner(0, d)), device_id_type=MESH
@@ -305,24 +306,20 @@
     bias_row = jnp.concatenate([bias[...] * 0.5] * 4, 1)
     slabs = 2 * CHUNK
     size = slabs * 2 * FACE
-    gather([-1, 0])
-    for chunk in range(CHUNKS):
+
+    def convolved(chunk, ty):
         base = chunk * slabs
-        gather(range(base + 1, base + slabs + 1))
-        total = None
-        for ty in range(3):
-            window = jnp.concatenate(
-                [
-                    stack[ty, base + tx : base + tx + slabs].reshape(size, BAND)
-                    for tx in range(3)
-                ],
-                1,
-            )
-            part = jnp.dot(window, band[ty], preferred_element_type=F32)
-            if ty != 1:
-                part = pltpu.roll(part.reshape(size // 8, 8, HALF), 1 if ty == 0 else 7, 1)
-                part = part.reshape(size, HALF)
-            total = part if total is None else total + part
+        window = jnp.concatenate(
+            [stack[ty, base + tx : base + tx + slabs].reshape(size, BAND) for tx in range(3)], 1
+        )
+        part = jnp.dot(window, band[ty], preferred_element_type=F32)
+        if ty != 1:
+            part = pltpu.roll(part.reshape(size // 8, 8, HALF), 1 if ty == 0 else 7, 1)
+            part = part.reshape(size, HALF)
+        return part
+
+    def reduced(chunk, total):
+        base = chunk * slabs
         half_v = total + bias_row
         own = stack[1, base + 1 : base + 1 + slabs, :, :, 0:HALF].reshape(size, HALF)
         hidden = own.astype(F32) + (half_v + half_v * jnp.tanh(half_v))
@@ -337,23 +334,48 @@
         coarse = jnp.dot(lhs, down_both[...], preferred_element_type=F32)
         odd = pltpu.roll(coarse[:, CO:].reshape(-1, 8, CO), 7, 1).reshape(-1, CO)
         coarse = (coarse[:, :CO] + odd).astype(BF16).reshape(2, CHUNK, 2, FACE, CO)
-        coarse = jnp.concatenate(
+        return jnp.concatenate(
             [coarse[k, :, h] for h in range(2) for k in range(2)], 2
         ).reshape(CHUNK * FACE, 4 * CO)
+
+    def staged(chunk, coarse):
         placed = jnp.dot(place[...], coarse, preferred_element_type=F32)
         placed = placed.reshape(2 * size_y, CHUNK, 8, 4 * CO)[:, :, 0:4]
         stage[chunk] = placed.astype(BF16)
-        for steps in straight:
-            out_copy(chunk, steps).start()
+
+    def send(chunk):
         if chunk == 0:
             pl.semaphore_wait(known_sem, SIDE - 1)
-        for steps in turning:
+        for steps in turning + straight:
             out_copy(chunk, steps).start()
         own_copy(chunk).start()
+
+    gather([-1, 0])
+    for chunk in range(CHUNKS):
+        gather(range(chunk * slabs + 1, chunk * slabs + slabs + 1))
+        total = convolved(chunk, 0) + convolved(chunk, 1) + convolved(chunk, 2)
+        staged(chunk, reduced(chunk, total))
+        send(chunk)
     for chunk in range(CHUNKS):
         for steps in straight + turning:
             out_copy(chunk, steps).wait()
         own_copy(chunk).wait()
+
+
+def hand_over(source, target, held, in_sem, out_sem):
+    size = source.shape[0] // PARTS
+    ins, outs = [], []
+    for k in range(PARTS):
+        part = pl.ds(k * size, size)
+        ins.append(pltpu.make_async_copy(source.at[part], held.at[part], in_sem.at[k]))
+        outs.append(pltpu.make_async_copy(held.at[part], target.at[part], out_sem.at[k]))
+    for copy in ins:
+        copy.start()
+    for arrived, leaving in zip(ins, outs):
+        arrived.wait()
+        leaving.start()
+    for copy in outs:
+        copy.wait()
 
 
 def shards(features, neighbour_ids, conv_weight, conv_bias, down_weight, coarse_owner):
@@ -361,7 +383,7 @@
     size_y = lax.axis_size("by")
     slots = 2 * size_y
     hbm_spec = pl.BlockSpec(memory_space=pltpu.HBM)
-    return pl.pallas_call(
+    out = pl.pallas_call(
         functools.partial(kernel, size_x, size_y),
         out_shape=jax.ShapeDtypeStruct((slots, 4, 4, 4 * CO), BF16),
         in_specs=[hbm_spec] * 6,
@@ -406,6 +428,19 @@
         conv_bias.reshape(1, CH),
         down_weight,
     )
+    return pl.pallas_call(
+        hand_over,
+        out_shape=jax.ShapeDtypeStruct(out.shape, out.dtype),
+        in_specs=[pl.BlockSpec(memory_space=pl.ANY)],
+        out_specs=pl.BlockSpec(memory_space=pl.ANY),
+        scratch_shapes=[
+            pltpu.VMEM(out.shape, out.dtype),
+            pltpu.SemaphoreType.DMA((PARTS,)),
+            pltpu.SemaphoreType.DMA((PARTS,)),
+        ],
+        compiler_params=pltpu.CompilerParams(vmem_limit_bytes=63 * 1024 * 1024),
+        name="hand_over",
+    )(out)
 
 
 def solution(mesh):

time: 25.5 us -> 24.7 us (0.969); the launches traced: 25.1 us -> 24.6 us
  local copies, waits for them, and re-layouts: 2.06 us -> 0 us
  Pallas kernels: 23 us -> 24.6 us
    unnamed x1 -> x0, local copies, waits for them, and re-layouts: 2.06 us -> none
    pallas_call x0 -> x1, Pallas kernels: none -> 1.82 us  [shards(): pl.pallas_call(hand_over, out_shape=jax.ShapeDtypeStruct(out.shape, out.d...]
    pallas_call x1, Pallas kernels: 23 us -> 22.7 us  [shards(): pl.pallas_call(functools.partial(kernel, size_x, size_y), out_shape=jax.S...]
where the time goes in v5:
time: 24.7 us; the launch traced here: 24.6 us
  Pallas kernels  24.6 us (100%)
    pallas_call x1, Pallas kernels, shards(): pl.pallas_call(functools.partial(kernel, size_x, size_y), out_shape=jax.S...  22.7 us
    pallas_call x1, Pallas kernels, shards(): pl.pallas_call(hand_over, out_shape=jax.ShapeDtypeStruct(out.shape, out.d...  1.82 us

profile of v5, /device:TPU:0, one launch (start us, length us, event | category | flops | bytes accessed | tf_op | source)
XLA Modules:
  0.0 24.6 jit_solution(10469622412318217203)
XLA Ops:
  0.0 22.7 %brick_encoder.1.source = bf16[32,4,4,512]{3,2,1,0:T(4,128)(2,1)} custom-call(s32[8,27]{1,0:T(8,128)} %ids_hbm.1, s32[1,8]{1,0:T(1,128)} %bitcast.4, bf16[512,512]{1,0:T(8,128)(2,1)} %bitcast.3, bf16[27,64,64]{2,1,0:T(8,128)(2,1)} %conv_hbm.1, f32[1,64]{1,0:T(1,128)} %bitcast.5, bf16[8,64,128]{2,1,0:T(8,128)(2,1)} %down_hbm.1), custom_call_target="tpu_custom_call" | custom-call | tf_op jit(solution)/shard_map/brick_encoder/pallas_call | solution.py:386
  22.8 1.8 %hand_over.1 = bf16[32,4,4,512]{3,2,1,0:T(4,128)(2,1)} custom-call(bf16[32,4,4,512]{3,2,1,0:T(4,128)(2,1)} %brick_encoder.1.source), custom_call_target="tpu_custom_call" | custom-call | tf_op jit(solution)/shard_map/hand_over/pallas_call | solution.py:431

commit v6 on v5

--- a/solution.py
+++ b/solution.py
@@ -71,7 +71,7 @@
     out_ref,
     ids, owner, feat, conv, bias, down,
     index, face_send, edge_send, face_recv, edge_recv, table, ytab, etab,
-    stack, band, down_both, place, stage,
+    stack, outer, lines, columns, acc, band, down_both, place, spread, stage,
     load_sem, halo_send, halo_recv, out_send, out_recv, own_sem, known_sem,
 ):
     i = lax.axis_index("bx")
@@ -154,32 +154,31 @@
 
     table[0:T_FACE] = feat[...].astype(F32).reshape(T_FACE, EDGE, LANES)
     table[T_ZERO:T_SIZE] = jnp.zeros((EDGE, EDGE, LANES), F32)
-    for k in range(2):
-        ytab[k, 0:BRICKS] = picked[(2 + k) * FACE : (3 + k) * FACE].reshape(BRICKS, EDGE, LANES)
-        ytab[k, Y_ZERO] = jnp.zeros((EDGE, LANES), F32)
-    for k in range(4):
-        repeat_rows(etab, k, 0, picked, 4 * FACE + k * BRICKS)
-        etab[k, E_ZERO] = jnp.zeros((EDGE, LANES), F32)
-
     loads[2].wait()
-    for g in range(BRICKS):
-        for tap in range(27):
-            sx, sy = tap // 9 - 1, tap // 3 % 3 - 1
-            value = ids[g, tap]
-            brick = value & 7
-            far_x = jnp.where(value >> 3 >> 4 == i, 0, 1)
-            far_y = jnp.where((value >> 3) & 15 == j, 0, 1)
-            if sx == 0 and sy == 0:
-                row, zero = brick * EDGE, T_ZERO
-            elif sy == 0:
-                edge_x, side = (7, 0) if sx < 0 else (0, 1)
-                row = jnp.where(far_x == 0, brick * EDGE + edge_x, T_FACE + side * BRICKS + brick)
-                zero = T_ZERO
-            elif sx == 0:
-                row, zero = far_y * BRICKS + brick, Y_ZERO
-            else:
-                row, zero = far_x * 16 + far_y * 8 + brick, E_ZERO
-            index[g, tap] = jnp.where(value >= 0, row, zero)
+
+    def locate(bricks, taps):
+        for g in bricks:
+            for tap in taps:
+                sx, sy = tap // 9 - 1, tap // 3 % 3 - 1
+                value = ids[g, tap]
+                brick = value & 7
+                far_x = jnp.where(value >> 3 >> 4 == i, 0, 1)
+                far_y = jnp.where((value >> 3) & 15 == j, 0, 1)
+                if sx == 0 and sy == 0:
+                    row, zero = brick * EDGE, T_ZERO
+                elif sy == 0:
+                    edge_x, side = (7, 0) if sx < 0 else (0, 1)
+                    row = jnp.where(
+                        far_x == 0, brick * EDGE + edge_x, T_FACE + side * BRICKS + brick
+                    )
+                    zero = T_ZERO
+                elif sx == 0:
+                    row, zero = far_y * BRICKS + brick, Y_ZERO
+                else:
+                    row, zero = far_x * 16 + far_y * 8 + brick, E_ZERO
+                index[g, tap] = jnp.where(value >= 0, row, zero)
+
+    locate(range(BRICKS), (12, 14))
 
     loads[1].wait()
     empty = jnp.zeros((CH, CH), BF16)
@@ -206,6 +205,73 @@
                 first = (a * 2 + k) * CH
                 down_both[first : first + CH, b * CO : (b + 1) * CO] = down[a * 4 + b * 2 + k]
 
+    low = iota((EDGE, 128), 1) < CH
+
+    def halves(c, m, p):
+        e0 = jnp.where(low, c[:, 256:384], m)
+        e1 = jnp.where(low, p, c[:, 128:256])
+        return (
+            jnp.concatenate([c[:, 0:256], e0], 1),
+            jnp.concatenate([c[:, 256:512], e1], 1),
+        )
+
+    def local_slab(g, x):
+        return halves(
+            table[g * EDGE + x],
+            table[index[g, 12] + x, :, LANES - 128 : LANES],
+            table[index[g, 14] + x, :, 0:128],
+        )
+
+    stack[0] = jnp.zeros((2, FACE, BAND), BF16)
+    stack[9] = jnp.zeros((2, FACE, BAND), BF16)
+    for k in range(2):
+        columns[k, 0] = jnp.zeros((16, BAND), BF16)
+        columns[k, 9] = jnp.zeros((16, BAND), BF16)
+
+    def gather_local(slabs):
+        for x in slabs:
+            for pair in range(BRICKS // 2):
+                even, odd = local_slab(pair * 2, x), local_slab(pair * 2 + 1, x)
+                for h in range(2):
+                    both = jnp.concatenate([even[h], odd[h]], 0)
+                    stack[x + 1, h, pair * 16 : pair * 16 + 16] = both.astype(BF16)
+
+    def windows(source, first, count, rows):
+        return jnp.concatenate(
+            [source[first + tx : first + tx + count].reshape(rows, BAND) for tx in range(3)], 1
+        )
+
+    def shifted(part, ty):
+        if ty == 1:
+            return part
+        moved = pltpu.roll(part.reshape(-1, 8, HALF), 1 if ty == 0 else 7, 1)
+        return moved.reshape(part.shape)
+
+    def convolve_local(first, count):
+        rows = count * 2 * FACE
+        window = windows(stack, first, count, rows)
+        y_of = iota((rows, HALF), 0) & 7
+        total = jnp.dot(window, band[1], preferred_element_type=F32)
+        for ty, empty in ((0, 0), (2, 7)):
+            part = jnp.dot(window, band[ty], preferred_element_type=F32)
+            total = total + jnp.where(y_of == empty, 0.0, shifted(part, ty))
+        acc[first : first + count] = total.reshape(count, 2, FACE, HALF)
+
+    rest = [tap for tap in range(27) if tap not in (12, 13, 14)]
+    gather_local(range(0, 5))
+    convolve_local(0, 4)
+    locate(range(0, 4), rest)
+    gather_local(range(5, 8))
+    convolve_local(4, 4)
+    locate(range(4, 8), rest)
+
+    for k in range(2):
+        ytab[k, 0:BRICKS] = picked[(2 + k) * FACE : (3 + k) * FACE].reshape(BRICKS, EDGE, LANES)
+        ytab[k, Y_ZERO] = jnp.zeros((EDGE, LANES), F32)
+    for k in range(4):
+        repeat_rows(etab, k, 0, picked, 4 * FACE + k * BRICKS)
+        etab[k, E_ZERO] = jnp.zeros((EDGE, LANES), F32)
+
     loads[3].wait()
     owners = [owner[0, g] for g in range(BRICKS)]
     row, col = iota((8 * CHUNK, FACE * CHUNK), 0), iota((8 * CHUNK, FACE * CHUNK), 1)
@@ -218,6 +284,16 @@
     slot_of = jnp.where((col >> 6 == row >> 3) & (col & 7 == (row & 7) * 2), slot_of, -1)
     blocks = [(slot_of == s).astype(F32) for s in range(2 * size_y)]
     place[...] = jnp.concatenate(blocks, 0).astype(BF16)
+
+    row, col = iota((128, 128), 0), iota((128, 128), 1)
+    turned = ((row >> 3) & 1) * 64 + (row & 7) * 8 + (row >> 4) == col
+    turned = turned.astype(F32).astype(BF16)
+    count = 2 * CHUNK * 16
+    row, col = iota((count * 8, count * 4), 0), iota((count * 8, count * 4), 1)
+    wanted = (col // (2 * count)) * 7
+    spread[...] = (
+        ((row >> 3 == lax.rem(col, count)) & (row & 7 == wanted)).astype(F32).astype(BF16)
+    )
 
     loads[4].wait()
     for copy, sent, received in copies:
@@ -237,53 +313,86 @@
             edge = jnp.concatenate([edge[0:8], edge[8:16]], 1)
             repeat_rows(etab, k * 2 + side, 24, edge)
 
-    low = iota((EDGE, 128), 1) < CH
     last_row = iota((EDGE, BAND), 0) == 7
     first_row = iota((EDGE, BAND), 0) == 0
 
-    def halves(read, centre, minus, plus):
-        c = read(centre, 0, LANES)
-        m = read(minus, LANES - 128, LANES)
-        p = read(plus, 0, 128)
-        e0 = jnp.where(low, c[:, 256:384], m)
-        e1 = jnp.where(low, p, c[:, 128:256])
-        return (
-            jnp.concatenate([c[:, 0:256], e0], 1),
-            jnp.concatenate([c[:, 256:512], e1], 1),
-        )
-
-    def one_slab(g, x):
-        sx = -1 if x < 0 else (1 if x > 7 else 0)
-        shift = x if sx == 0 else 0
+    def outer_slab(g, side):
+        sx = side * 2 - 1
         result = []
         for sy in STEPS:
             tap = (sx + 1) * 9 + (sy + 1) * 3
-            if sy == 0:
-                def read(row, low_lane, high_lane):
-                    return table[row + shift, :, low_lane:high_lane]
-            elif sx == 0:
-                def read(row, low_lane, high_lane, side=(sy + 1) // 2):
-                    lines = ytab[side, row, :, low_lane:high_lane]
-                    return pltpu.roll(lines, (7 - x if side == 0 else 0 - x) & 7, 0)
-            else:
-                def read(row, low_lane, high_lane, corner=(sx + 1) // 2 * 2 + (sy + 1) // 2):
-                    return etab[corner, row, :, low_lane:high_lane]
-            result.append(halves(read, index[g, tap + 1], index[g, tap], index[g, tap + 2]))
+            source = table if sy == 0 else etab.at[side * 2 + (sy + 1) // 2]
+            result.append(
+                halves(
+                    source[index[g, tap + 1]],
+                    source[index[g, tap], :, LANES - 128 : LANES],
+                    source[index[g, tap + 2], :, 0:128],
+                )
+            )
         before, same, after = result
         return [
-            [jnp.where(last_row, before[h], same[h]), same[h], jnp.where(first_row, after[h], same[h])]
+            [
+                jnp.where(last_row, before[h], same[h]),
+                same[h],
+                jnp.where(first_row, after[h], same[h]),
+            ]
             for h in range(2)
         ]
 
-    def gather(slabs):
-        for x in slabs:
-            for pair in range(BRICKS // 2):
-                even = one_slab(pair * 2, x)
-                odd = one_slab(pair * 2 + 1, x)
-                for h in range(2):
-                    for ty in range(3):
-                        both = jnp.concatenate([even[h][ty], odd[h][ty]], 0)
-                        stack[ty, x + 1, h, pair * 16 : pair * 16 + 16] = both.astype(BF16)
+    def line(g, side):
+        tap = 9 + side * 6
+        return halves(
+            ytab[side, index[g, tap + 1]],
+            ytab[side, index[g, tap], :, LANES - 128 : LANES],
+            ytab[side, index[g, tap + 2], :, 0:128],
+        )
+
+    for side in range(2):
+        for pair in range(BRICKS // 2):
+            even, odd = line(pair * 2, side), line(pair * 2 + 1, side)
+            for h in range(2):
+                first = h * FACE + pair * 16
+                both = jnp.concatenate([even[h], odd[h]], 0)
+                lines[side, first : first + 16] = both.astype(BF16)
+    for side in range(2):
+        moved = jnp.dot(turned, lines[side], preferred_element_type=F32)
+        columns[side, 1:9] = moved.astype(BF16).reshape(8, 16, BAND)
+    for side in range(2):
+        for pair in range(BRICKS // 2):
+            even, odd = outer_slab(pair * 2, side), outer_slab(pair * 2 + 1, side)
+            for h in range(2):
+                for ty in range(3):
+                    both = jnp.concatenate([even[h][ty], odd[h][ty]], 0)
+                    outer[side, ty, h, pair * 16 : pair * 16 + 16] = both.astype(BF16)
+    terms = []
+    for side in range(2):
+        window = windows(columns.at[side], 0, 8, 128)
+        value = jnp.dot(window, band[side * 2], preferred_element_type=F32)
+        high = value.astype(BF16)
+        terms.append((high, (value - high.astype(F32)).astype(BF16)))
+    for side in range(2):
+        extra = None
+        for ty in range(3):
+            first = side * 2 * BAND
+            part = jnp.dot(
+                outer[side, ty].reshape(2 * FACE, BAND),
+                band[ty, first : first + BAND],
+                preferred_element_type=F32,
+            )
+            part = shifted(part, ty)
+            extra = part if extra is None else extra + part
+        acc[side * 7] = acc[side * 7] + extra.reshape(2, FACE, HALF)
+
+    def convolved(chunk):
+        first = chunk * count
+        part = jnp.concatenate(
+            [term[first : first + count] for pair in terms for term in pair], 0
+        )
+        total = acc[chunk * slabs : chunk * slabs + slabs].reshape(size, HALF)
+        return total + jnp.dot(spread[...], part, preferred_element_type=F32)
+
+    slabs = 2 * CHUNK
+    size = slabs * 2 * FACE
 
     def out_copy(chunk, steps):
         dest = partner(*steps)
@@ -304,24 +413,10 @@
         )
 
     bias_row = jnp.concatenate([bias[...] * 0.5] * 4, 1)
-    slabs = 2 * CHUNK
-    size = slabs * 2 * FACE
-
-    def convolved(chunk, ty):
-        base = chunk * slabs
-        window = jnp.concatenate(
-            [stack[ty, base + tx : base + tx + slabs].reshape(size, BAND) for tx in range(3)], 1
-        )
-        part = jnp.dot(window, band[ty], preferred_element_type=F32)
-        if ty != 1:
-            part = pltpu.roll(part.reshape(size // 8, 8, HALF), 1 if ty == 0 else 7, 1)
-            part = part.reshape(size, HALF)
-        return part
-
     def reduced(chunk, total):
         base = chunk * slabs
         half_v = total + bias_row
-        own = stack[1, base + 1 : base + 1 + slabs, :, :, 0:HALF].reshape(size, HALF)
+        own = stack[base + 1 : base + 1 + slabs, :, :, 0:HALF].reshape(size, HALF)
         hidden = own.astype(F32) + (half_v + half_v * jnp.tanh(half_v))
         hidden = hidden.astype(BF16).reshape(CHUNK, 2, 2 * FACE, HALF)
         lhs = jnp.concatenate(
@@ -350,11 +445,8 @@
             out_copy(chunk, steps).start()
         own_copy(chunk).start()
 
-    gather([-1, 0])
     for chunk in range(CHUNKS):
-        gather(range(chunk * slabs + 1, chunk * slabs + slabs + 1))
-        total = convolved(chunk, 0) + convolved(chunk, 1) + convolved(chunk, 2)
-        staged(chunk, reduced(chunk, total))
+        staged(chunk, reduced(chunk, convolved(chunk)))
         send(chunk)
     for chunk in range(CHUNKS):
         for steps in straight + turning:
@@ -403,10 +495,15 @@
             pltpu.VMEM((T_SIZE, EDGE, LANES), F32),
             pltpu.VMEM((2, Y_SIZE, EDGE, LANES), F32),
             pltpu.VMEM((4, E_SIZE, EDGE, LANES), F32),
-            pltpu.VMEM((3, 10, 2, FACE, BAND), BF16),
+            pltpu.VMEM((10, 2, FACE, BAND), BF16),
+            pltpu.VMEM((2, 3, 2, FACE, BAND), BF16),
+            pltpu.VMEM((2, 2 * FACE, BAND), BF16),
+            pltpu.VMEM((2, 10, 16, BAND), BF16),
+            pltpu.VMEM((EDGE, 2, FACE, HALF), F32),
             pltpu.VMEM((3, 3 * BAND, HALF), BF16),
             pltpu.VMEM((256, 2 * CO), BF16),
             pltpu.VMEM((slots * 8 * CHUNK, FACE * CHUNK), BF16),
+            pltpu.VMEM((256 * CHUNK, 128 * CHUNK), BF16),
             pltpu.VMEM((CHUNKS, slots, CHUNK, 4, 4 * CO), BF16),
             pltpu.SemaphoreType.DMA((6,)),
             pltpu.SemaphoreType.DMA((8,)),

time: 24.7 us -> 23.8 us (0.964)
  Pallas kernels: 24.6 us -> 23.7 us
    pallas_call x1, Pallas kernels: 22.7 us -> 21.9 us  [shards(): pl.pallas_call(functools.partial(kernel, size_x, size_y), out_shape=jax.S...]
where the time goes in v6:
time: 23.8 us; the launch traced here: 23.7 us
  Pallas kernels  23.7 us (100%)
    pallas_call x1, Pallas kernels, shards(): pl.pallas_call(functools.partial(kernel, size_x, size_y), out_shape=jax.S...  21.9 us
    pallas_call x1, Pallas kernels, shards(): pl.pallas_call(hand_over, out_shape=jax.ShapeDtypeStruct(out.shape, out.d...  1.82 us

profile of v6, /device:TPU:0, one launch (start us, length us, event | category | flops | bytes accessed | tf_op | source)
XLA Modules:
  0.0 23.7 jit_solution(9650163147322756595)
XLA Ops:
  0.0 21.9 %brick_encoder.1.source = bf16[32,4,4,512]{3,2,1,0:T(4,128)(2,1)} custom-call(s32[8,27]{1,0:T(8,128)} %ids_hbm.1, s32[1,8]{1,0:T(1,128)} %bitcast.4, bf16[512,512]{1,0:T(8,128)(2,1)} %bitcast.3, bf16[27,64,64]{2,1,0:T(8,128)(2,1)} %conv_hbm.1, f32[1,64]{1,0:T(1,128)} %bitcast.5, bf16[8,64,128]{2,1,0:T(8,128)(2,1)} %down_hbm.1), custom_call_target="tpu_custom_call" | custom-call | tf_op jit(solution)/shard_map/brick_encoder/pallas_call | solution.py:478
  21.9 1.8 %hand_over.1 = bf16[32,4,4,512]{3,2,1,0:T(4,128)(2,1)} custom-call(bf16[32,4,4,512]{3,2,1,0:T(4,128)(2,1)} %brick_encoder.1.source), custom_call_target="tpu_custom_call" | custom-call | tf_op jit(solution)/shard_map/hand_over/pallas_call | solution.py:528

commit v7 on v6

--- a/solution.py
+++ b/solution.py
@@ -32,8 +32,8 @@
 STEPS = (-1, 0, 1)
 CHUNK = 2
 CHUNKS = EDGE // 2 // CHUNK
+ORDER = (1, 2, 0, 3)
 SIDE = 4
-PARTS = 4
 HALO = [(1, 0), (-1, 0), (0, 1), (0, -1), (1, 1), (1, -1), (-1, 1), (-1, -1)]
 
 
@@ -101,15 +101,11 @@
     def partner(step_z, step_y):
         return lax.rem(z + step_z, SIDE) * SIDE + lax.rem(y + step_y, SIDE)
 
-    straight = [(0, d) for d in range(1, SIDE)] + [(d, 0) for d in range(1, SIDE)]
-    turning = [(a, b) for a in range(1, SIDE) for b in range(1, SIDE)]
+    straight = [(0, 1), (0, 3), (1, 0), (3, 0), (0, 2), (2, 0)]
+    turning = [(1, 1), (3, 3), (1, 2), (3, 2), (2, 2), (2, 1), (2, 3), (1, 3), (3, 1)]
 
     barrier = pltpu.get_barrier_semaphore()
-    for steps in straight:
-        pl.semaphore_signal(
-            barrier, inc=1, device_id=(i, partner(*steps)), device_id_type=MESH
-        )
-    greetings = jnp.int32(len(straight))
+    greetings = j
     for step_x, step_y in HALO:
         here = inside(step_x, step_y)
         greetings = greetings + jnp.where(here, 1, 0)
@@ -119,6 +115,12 @@
             pl.semaphore_signal(
                 barrier, inc=1, device_id=(i + step_x, j + step_y), device_id_type=MESH
             )
+
+    for d in range(1, size_y):
+
+        @pl.when(j + d < size_y)
+        def _(d=d):
+            pl.semaphore_signal(barrier, inc=1, device_id=(i, j + d), device_id_type=MESH)
 
     pick = picked_rows()
     loads[0].wait()
@@ -145,12 +147,14 @@
             device_id_type=MESH,
         )
         copies.append((copy, inside(step_x, step_y), inside(-step_x, -step_y)))
-    for copy, sent, received in copies[4:] + copies[2:4] + copies[:2]:
+    for copy, sent, received in copies[2:4] + copies[4::3] + copies[5:7] + copies[:2]:
         pl.when(sent)(copy.start)
-    for d in range(1, SIDE):
-        pl.semaphore_signal(
-            known_sem, inc=1, device_id=(i, partner(0, d)), device_id_type=MESH
-        )
+
+    for d in range(1, size_y):
+
+        @pl.when(j >= d)
+        def _(d=d):
+            pl.semaphore_signal(known_sem, inc=1, device_id=(i, j - d), device_id_type=MESH)
 
     table[0:T_FACE] = feat[...].astype(F32).reshape(T_FACE, EDGE, LANES)
     table[T_ZERO:T_SIZE] = jnp.zeros((EDGE, EDGE, LANES), F32)
@@ -296,18 +300,122 @@
     )
 
     loads[4].wait()
-    for copy, sent, received in copies:
-        pl.when(sent)(copy.wait_send)
-        pl.when(received)(copy.wait_recv)
+
+    def arrive(some):
+        for copy, sent, received in some:
+            pl.when(sent)(copy.wait_send)
+            pl.when(received)(copy.wait_recv)
+
+    arrive(copies[2:4])
+    over_y = [face_recv[2 + k].astype(F32) for k in range(2)]
+    for k in range(2):
+        ytab[k, BRICKS : 2 * BRICKS] = over_y[k].reshape(BRICKS, EDGE, LANES)
+
+    def line(g, side):
+        tap = 9 + side * 6
+        return halves(
+            ytab[side, index[g, tap + 1]],
+            ytab[side, index[g, tap], :, LANES - 128 : LANES],
+            ytab[side, index[g, tap + 2], :, 0:128],
+        )
+
+    for side in range(2):
+        for pair in range(BRICKS // 2):
+            even, odd = line(pair * 2, side), line(pair * 2 + 1, side)
+            for h in range(2):
+                first = h * FACE + pair * 16
+                both = jnp.concatenate([even[h], odd[h]], 0)
+                lines[side, first : first + 16] = both.astype(BF16)
+    for side in range(2):
+        moved = jnp.dot(turned, lines[side], preferred_element_type=F32)
+        columns[side, 1:9] = moved.astype(BF16).reshape(8, 16, BAND)
+    terms = []
+    for side in range(2):
+        window = windows(columns.at[side], 0, 8, 128)
+        value = jnp.dot(window, band[side * 2], preferred_element_type=F32)
+        high = value.astype(BF16)
+        terms.append((high, (value - high.astype(F32)).astype(BF16)))
+    def order(chunk):
+        return ORDER[chunk * CHUNK : chunk * CHUNK + CHUNK]
+
+    def convolved(chunk):
+        part = jnp.concatenate(
+            [term[32 * k : 32 * k + 32] for pair in terms for term in pair for k in order(chunk)],
+            0,
+        )
+        total = jnp.concatenate([acc[2 * k : 2 * k + 2] for k in order(chunk)], 0)
+        return total.reshape(size, HALF) + jnp.dot(spread[...], part, preferred_element_type=F32)
+
+    slabs = 2 * CHUNK
+    size = slabs * 2 * FACE
+
+    def out_copy(chunk, steps):
+        dest = partner(*steps)
+        return pltpu.make_async_remote_copy(
+            src_ref=stage.at[chunk, pl.ds(dest * 2, 2)],
+            dst_ref=out_ref.at[pl.ds(j * 2, 2), pl.ds(chunk * CHUNK, CHUNK)],
+            send_sem=out_send.at[chunk, steps[0] * SIDE + steps[1]],
+            recv_sem=out_recv.at[chunk, steps[0] * SIDE + steps[1]],
+            device_id=(i, dest),
+            device_id_type=MESH,
+        )
+
+    def own_copy(chunk):
+        return pltpu.make_async_copy(
+            stage.at[chunk, pl.ds(j * 2, 2)],
+            out_ref.at[pl.ds(j * 2, 2), pl.ds(chunk * CHUNK, CHUNK)],
+            own_sem.at[chunk],
+        )
+
+    bias_row = jnp.concatenate([bias[...] * 0.5] * 4, 1)
+    def reduced(chunk, total):
+        half_v = total + bias_row
+        own = jnp.concatenate(
+            [stack[2 * k + 1 : 2 * k + 3, :, :, 0:HALF] for k in order(chunk)], 0
+        ).reshape(size, HALF)
+        hidden = own.astype(F32) + (half_v + half_v * jnp.tanh(half_v))
+        hidden = hidden.astype(BF16).reshape(CHUNK, 2, 2 * FACE, HALF)
+        lhs = jnp.concatenate(
+            [
+                jnp.concatenate([hidden[:, a, :, k * 128 : (k + 1) * 128] for a in range(2)], 2)
+                for k in range(2)
+            ],
+            0,
+        ).reshape(2 * CHUNK * 2 * FACE, 256)
+        coarse = jnp.dot(lhs, down_both[...], preferred_element_type=F32)
+        odd = pltpu.roll(coarse[:, CO:].reshape(-1, 8, CO), 7, 1).reshape(-1, CO)
+        coarse = (coarse[:, :CO] + odd).astype(BF16).reshape(2, CHUNK, 2, FACE, CO)
+        return jnp.concatenate(
+            [coarse[k, :, h] for h in range(2) for k in range(2)], 2
+        ).reshape(CHUNK * FACE, 4 * CO)
+
+    def staged(chunk, coarse):
+        placed = jnp.dot(place[...], coarse, preferred_element_type=F32)
+        placed = placed.reshape(2 * size_y, CHUNK, 8, 4 * CO)[:, :, 0:4]
+        stage[chunk] = placed.astype(BF16)
+
+    def send(chunk):
+        if chunk == 0:
+
+            @pl.when(j + 1 < size_y)
+            def _():
+                pl.semaphore_wait(known_sem, size_y - 1 - j)
+
+        for steps in turning + straight:
+            out_copy(chunk, steps).start()
+        own_copy(chunk).start()
+
+    staged(0, reduced(0, convolved(0)))
+    send(0)
+
+    arrive(copies[:2] + copies[4:])
     for k in range(2):
         over_x = face_recv[k].astype(F32)
-        over_y = face_recv[2 + k].astype(F32)
         first = T_FACE + k * BRICKS
         table[first : first + BRICKS] = over_x.reshape(BRICKS, EDGE, LANES)
-        ytab[k, BRICKS : 2 * BRICKS] = over_y.reshape(BRICKS, EDGE, LANES)
         for side in range(2):
             at = 0 if side else 7
-            repeat_rows(etab, side * 2 + k, 8, over_y, at, EDGE)
+            repeat_rows(etab, side * 2 + k, 8, over_y[k], at, EDGE)
             repeat_rows(etab, k * 2 + side, 16, over_x, at, EDGE)
             edge = edge_recv[k * 2 + side].astype(F32)
             edge = jnp.concatenate([edge[0:8], edge[8:16]], 1)
@@ -339,24 +447,6 @@
             for h in range(2)
         ]
 
-    def line(g, side):
-        tap = 9 + side * 6
-        return halves(
-            ytab[side, index[g, tap + 1]],
-            ytab[side, index[g, tap], :, LANES - 128 : LANES],
-            ytab[side, index[g, tap + 2], :, 0:128],
-        )
-
-    for side in range(2):
-        for pair in range(BRICKS // 2):
-            even, odd = line(pair * 2, side), line(pair * 2 + 1, side)
-            for h in range(2):
-                first = h * FACE + pair * 16
-                both = jnp.concatenate([even[h], odd[h]], 0)
-                lines[side, first : first + 16] = both.astype(BF16)
-    for side in range(2):
-        moved = jnp.dot(turned, lines[side], preferred_element_type=F32)
-        columns[side, 1:9] = moved.astype(BF16).reshape(8, 16, BAND)
     for side in range(2):
         for pair in range(BRICKS // 2):
             even, odd = outer_slab(pair * 2, side), outer_slab(pair * 2 + 1, side)
@@ -364,12 +454,6 @@
                 for ty in range(3):
                     both = jnp.concatenate([even[h][ty], odd[h][ty]], 0)
                     outer[side, ty, h, pair * 16 : pair * 16 + 16] = both.astype(BF16)
-    terms = []
-    for side in range(2):
-        window = windows(columns.at[side], 0, 8, 128)
-        value = jnp.dot(window, band[side * 2], preferred_element_type=F32)
-        high = value.astype(BF16)
-        terms.append((high, (value - high.astype(F32)).astype(BF16)))
     for side in range(2):
         extra = None
         for ty in range(3):
@@ -383,71 +467,8 @@
             extra = part if extra is None else extra + part
         acc[side * 7] = acc[side * 7] + extra.reshape(2, FACE, HALF)
 
-    def convolved(chunk):
-        first = chunk * count
-        part = jnp.concatenate(
-            [term[first : first + count] for pair in terms for term in pair], 0
-        )
-        total = acc[chunk * slabs : chunk * slabs + slabs].reshape(size, HALF)
-        return total + jnp.dot(spread[...], part, preferred_element_type=F32)
-
-    slabs = 2 * CHUNK
-    size = slabs * 2 * FACE
-
-    def out_copy(chunk, steps):
-        dest = partner(*steps)
-        return pltpu.make_async_remote_copy(
-            src_ref=stage.at[chunk, pl.ds(dest * 2, 2)],
-            dst_ref=out_ref.at[pl.ds(j * 2, 2), pl.ds(chunk * CHUNK, CHUNK)],
-            send_sem=out_send.at[chunk, steps[0] * SIDE + steps[1]],
-            recv_sem=out_recv.at[chunk, steps[0] * SIDE + steps[1]],
-            device_id=(i, dest),
-            device_id_type=MESH,
-        )
-
-    def own_copy(chunk):
-        return pltpu.make_async_copy(
-            stage.at[chunk, pl.ds(j * 2, 2)],
-            out_ref.at[pl.ds(j * 2, 2), pl.ds(chunk * CHUNK, CHUNK)],
-            own_sem.at[chunk],
-        )
-
-    bias_row = jnp.concatenate([bias[...] * 0.5] * 4, 1)
-    def reduced(chunk, total):
-        base = chunk * slabs
-        half_v = total + bias_row
-        own = stack[base + 1 : base + 1 + slabs, :, :, 0:HALF].reshape(size, HALF)
-        hidden = own.astype(F32) + (half_v + half_v * jnp.tanh(half_v))
-        hidden = hidden.astype(BF16).reshape(CHUNK, 2, 2 * FACE, HALF)
-        lhs = jnp.concatenate(
-            [
-                jnp.concatenate([hidden[:, a, :, k * 128 : (k + 1) * 128] for a in range(2)], 2)
-                for k in range(2)
-            ],
-            0,
-        ).reshape(2 * CHUNK * 2 * FACE, 256)
-        coarse = jnp.dot(lhs, down_both[...], preferred_element_type=F32)
-        odd = pltpu.roll(coarse[:, CO:].reshape(-1, 8, CO), 7, 1).reshape(-1, CO)
-        coarse = (coarse[:, :CO] + odd).astype(BF16).reshape(2, CHUNK, 2, FACE, CO)
-        return jnp.concatenate(
-            [coarse[k, :, h] for h in range(2) for k in range(2)], 2
-        ).reshape(CHUNK * FACE, 4 * CO)
-
-    def staged(chunk, coarse):
-        placed = jnp.dot(place[...], coarse, preferred_element_type=F32)
-        placed = placed.reshape(2 * size_y, CHUNK, 8, 4 * CO)[:, :, 0:4]
-        stage[chunk] = placed.astype(BF16)
-
-    def send(chunk):
-        if chunk == 0:
-            pl.semaphore_wait(known_sem, SIDE - 1)
-        for steps in turning + straight:
-            out_copy(chunk, steps).start()
-        own_copy(chunk).start()
-
-    for chunk in range(CHUNKS):
-        staged(chunk, reduced(chunk, convolved(chunk)))
-        send(chunk)
+    staged(1, reduced(1, convolved(1)))
+    send(1)
     for chunk in range(CHUNKS):
         for steps in straight + turning:
             out_copy(chunk, steps).wait()
@@ -455,12 +476,10 @@
 
 
 def hand_over(source, target, held, in_sem, out_sem):
-    size = source.shape[0] // PARTS
     ins, outs = [], []
-    for k in range(PARTS):
-        part = pl.ds(k * size, size)
-        ins.append(pltpu.make_async_copy(source.at[part], held.at[part], in_sem.at[k]))
-        outs.append(pltpu.make_async_copy(held.at[part], target.at[part], out_sem.at[k]))
+    for k, x in enumerate(ORDER):
+        ins.append(pltpu.make_async_copy(source.at[:, k], held.at[k], in_sem.at[k]))
+        outs.append(pltpu.make_async_copy(held.at[k], target.at[:, x], out_sem.at[k]))
     for copy in ins:
         copy.start()
     for arrived, leaving in zip(ins, outs):
@@ -531,9 +550,9 @@
         in_specs=[pl.BlockSpec(memory_space=pl.ANY)],
         out_specs=pl.BlockSpec(memory_space=pl.ANY),
         scratch_shapes=[
-            pltpu.VMEM(out.shape, out.dtype),
-            pltpu.SemaphoreType.DMA((PARTS,)),
-            pltpu.SemaphoreType.DMA((PARTS,)),
+            pltpu.VMEM((4, slots, 4, 4 * CO), out.dtype),
+            pltpu.SemaphoreType.DMA((4,)),
+            pltpu.SemaphoreType.DMA((4,)),
         ],
         compiler_params=pltpu.CompilerParams(vmem_limit_bytes=63 * 1024 * 1024),
         name="hand_over",

time: 23.8 us -> 23.2 us (0.975)
  Pallas kernels: 23.7 us -> 23.1 us
    pallas_call x1, Pallas kernels: 21.9 us -> 21.3 us  [shards(): pl.pallas_call(functools.partial(kernel, size_x, size_y), out_shape=jax.S...]
where the time goes in v7:
time: 23.2 us; the launch traced here: 23.1 us
  Pallas kernels  23.1 us (100%)
    pallas_call x1, Pallas kernels, shards(): pl.pallas_call(functools.partial(kernel, size_x, size_y), out_shape=jax.S...  21.3 us
    pallas_call x1, Pallas kernels, shards(): pl.pallas_call(hand_over, out_shape=jax.ShapeDtypeStruct(out.shape, out.d...  1.82 us

profile of v7, /device:TPU:0, one launch (start us, length us, event | category | flops | bytes accessed | tf_op | source)
XLA Modules:
  0.0 23.1 jit_solution(10818350162386135485)
XLA Ops:
  0.0 21.3 %brick_encoder.1.source = bf16[32,4,4,512]{3,2,1,0:T(4,128)(2,1)} custom-call(s32[8,27]{1,0:T(8,128)} %ids_hbm.1, s32[1,8]{1,0:T(1,128)} %bitcast.4, bf16[512,512]{1,0:T(8,128)(2,1)} %bitcast.3, bf16[27,64,64]{2,1,0:T(8,128)(2,1)} %conv_hbm.1, f32[1,64]{1,0:T(1,128)} %bitcast.5, bf16[8,64,128]{2,1,0:T(8,128)(2,1)} %down_hbm.1), custom_call_target="tpu_custom_call" | custom-call | tf_op jit(solution)/shard_map/brick_encoder/pallas_call | solution.py:497
  21.3 1.8 %hand_over.1 = bf16[32,4,4,512]{3,2,1,0:T(4,128)(2,1)} custom-call(bf16[32,4,4,512]{3,2,1,0:T(4,128)(2,1)} %brick_encoder.1.source), custom_call_target="tpu_custom_call" | custom-call | tf_op jit(solution)/shard_map/hand_over/pallas_call | solution.py:547

commit v8 on v7

--- a/solution.py
+++ b/solution.py
@@ -70,9 +70,9 @@
     ids_hbm, owner_hbm, feat_hbm, conv_hbm, bias_hbm, down_hbm,
     out_ref,
     ids, owner, feat, conv, bias, down,
-    index, face_send, edge_send, face_recv, edge_recv, table, ytab, etab,
+    located, index, face_send, edge_send, face_recv, edge_recv, table, ytab, etab,
     stack, outer, lines, columns, acc, band, down_both, place, spread, stage,
-    load_sem, halo_send, halo_recv, out_send, out_recv, own_sem, known_sem,
+    load_sem, locate_sem, halo_send, halo_recv, out_send, out_recv, own_sem, known_sem,
 ):
     i = lax.axis_index("bx")
     j = lax.axis_index("by")
@@ -130,6 +130,25 @@
         first = 4 * FACE + k * BRICKS
         edge = picked[first : first + BRICKS]
         edge_send[k] = jnp.concatenate([edge[:, 0:256], edge[:, 256:512]], 0).astype(BF16)
+
+    loads[2].wait()
+    value, tap = ids[...], iota((BRICKS, 27), 1)
+    sx = jnp.where(tap < 9, -1, jnp.where(tap < 18, 0, 1))
+    inner = tap - 9 * (sx + 1)
+    sy = jnp.where(inner < 3, -1, jnp.where(inner < 6, 0, 1))
+    brick = value & 7
+    far_x = jnp.where((value >> 7) == i, 0, 1)
+    far_y = jnp.where(((value >> 3) & 15) == j, 0, 1)
+    near = brick * EDGE + jnp.where(sx < 0, 7, 0)
+    far = T_FACE + jnp.where(sx < 0, 0, BRICKS) + brick
+    flat = jnp.where(sx == 0, brick * EDGE, jnp.where(far_x == 0, near, far))
+    bent = jnp.where(sx == 0, 0, far_x * 16) + far_y * 8 + brick
+    nothing = jnp.where(sx == 0, Y_ZERO, E_ZERO)
+    located[...] = jnp.where(
+        value >= 0, jnp.where(sy == 0, flat, bent), jnp.where(sy == 0, T_ZERO, nothing)
+    )
+    locating = pltpu.make_async_copy(located, index, locate_sem)
+    locating.start()
 
     pl.semaphore_wait(barrier, greetings)
     copies = []
@@ -158,32 +177,6 @@
 
     table[0:T_FACE] = feat[...].astype(F32).reshape(T_FACE, EDGE, LANES)
     table[T_ZERO:T_SIZE] = jnp.zeros((EDGE, EDGE, LANES), F32)
-    loads[2].wait()
-
-    def locate(bricks, taps):
-        for g in bricks:
-            for tap in taps:
-                sx, sy = tap // 9 - 1, tap // 3 % 3 - 1
-                value = ids[g, tap]
-                brick = value & 7
-                far_x = jnp.where(value >> 3 >> 4 == i, 0, 1)
-                far_y = jnp.where((value >> 3) & 15 == j, 0, 1)
-                if sx == 0 and sy == 0:
-                    row, zero = brick * EDGE, T_ZERO
-                elif sy == 0:
-                    edge_x, side = (7, 0) if sx < 0 else (0, 1)
-                    row = jnp.where(
-                        far_x == 0, brick * EDGE + edge_x, T_FACE + side * BRICKS + brick
-                    )
-                    zero = T_ZERO
-                elif sx == 0:
-                    row, zero = far_y * BRICKS + brick, Y_ZERO
-                else:
-                    row, zero = far_x * 16 + far_y * 8 + brick, E_ZERO
-                index[g, tap] = jnp.where(value >= 0, row, zero)
-
-    locate(range(BRICKS), (12, 14))
-
     loads[1].wait()
     empty = jnp.zeros((CH, CH), BF16)
     blank = jnp.zeros((CH, 2 * CH), BF16)
@@ -261,13 +254,11 @@
             total = total + jnp.where(y_of == empty, 0.0, shifted(part, ty))
         acc[first : first + count] = total.reshape(count, 2, FACE, HALF)
 
-    rest = [tap for tap in range(27) if tap not in (12, 13, 14)]
+    locating.wait()
     gather_local(range(0, 5))
     convolve_local(0, 4)
-    locate(range(0, 4), rest)
     gather_local(range(5, 8))
     convolve_local(4, 4)
-    locate(range(4, 8), rest)
 
     for k in range(2):
         ytab[k, 0:BRICKS] = picked[(2 + k) * FACE : (3 + k) * FACE].reshape(BRICKS, EDGE, LANES)
@@ -278,14 +269,14 @@
 
     loads[3].wait()
     owners = [owner[0, g] for g in range(BRICKS)]
-    row, col = iota((8 * CHUNK, FACE * CHUNK), 0), iota((8 * CHUNK, FACE * CHUNK), 1)
-    slot_of = jnp.zeros((8 * CHUNK, FACE * CHUNK), jnp.int32)
+    row, col = iota((4 * CHUNK, FACE * CHUNK), 0), iota((4 * CHUNK, FACE * CHUNK), 1)
+    slot_of = jnp.zeros((4 * CHUNK, FACE * CHUNK), jnp.int32)
     for g in range(BRICKS):
         rank = jnp.int32(0)
         for earlier in range(g):
             rank = rank + jnp.where(owners[earlier] == owners[g], 1, 0)
         slot_of = jnp.where((col >> 3) & 7 == g, owners[g] * 2 + rank, slot_of)
-    slot_of = jnp.where((col >> 6 == row >> 3) & (col & 7 == (row & 7) * 2), slot_of, -1)
+    slot_of = jnp.where((col >> 6 == row >> 2) & (col & 7 == (row & 3) * 2), slot_of, -1)
     blocks = [(slot_of == s).astype(F32) for s in range(2 * size_y)]
     place[...] = jnp.concatenate(blocks, 0).astype(BF16)
 
@@ -391,8 +382,9 @@
 
     def staged(chunk, coarse):
         placed = jnp.dot(place[...], coarse, preferred_element_type=F32)
-        placed = placed.reshape(2 * size_y, CHUNK, 8, 4 * CO)[:, :, 0:4]
-        stage[chunk] = placed.astype(BF16)
+        placed = placed.reshape(2 * size_y, 4 * CHUNK, 4 * CO)
+        for k in range(CHUNK):
+            stage[chunk, :, k] = placed[:, 4 * k : 4 * k + 4].astype(BF16)
 
     def send(chunk):
         if chunk == 0:
@@ -500,12 +492,13 @@
         in_specs=[hbm_spec] * 6,
         out_specs=pl.BlockSpec(memory_space=pl.ANY),
         scratch_shapes=[
-            pltpu.SMEM((BRICKS, 27), jnp.int32),
+            pltpu.VMEM((BRICKS, 27), jnp.int32),
             pltpu.SMEM((1, BRICKS), jnp.int32),
             pltpu.VMEM((ROWS, LANES), BF16),
             pltpu.VMEM((27, CH, CH), BF16),
             pltpu.VMEM((1, CH), F32),
             pltpu.VMEM((8, CH, CO), BF16),
+            pltpu.VMEM((BRICKS, 27), jnp.int32),
             pltpu.SMEM((BRICKS, 27), jnp.int32),
             pltpu.VMEM((4, FACE, LANES), BF16),
             pltpu.VMEM((4, 16, 256), BF16),
@@ -521,10 +514,11 @@
             pltpu.VMEM((EDGE, 2, FACE, HALF), F32),
             pltpu.VMEM((3, 3 * BAND, HALF), BF16),
             pltpu.VMEM((256, 2 * CO), BF16),
-            pltpu.VMEM((slots * 8 * CHUNK, FACE * CHUNK), BF16),
+            pltpu.VMEM((slots * 4 * CHUNK, FACE * CHUNK), BF16),
             pltpu.VMEM((256 * CHUNK, 128 * CHUNK), BF16),
             pltpu.VMEM((CHUNKS, slots, CHUNK, 4, 4 * CO), BF16),
             pltpu.SemaphoreType.DMA((6,)),
+            pltpu.SemaphoreType.DMA,
             pltpu.SemaphoreType.DMA((8,)),
             pltpu.SemaphoreType.DMA((8,)),
             pltpu.SemaphoreType.DMA((CHUNKS, size_y)),

time: 23.2 us -> 23.2 us (level)
  no operation moved by 1% of the time
where the time goes in v8:
time: 23.2 us; the launch traced here: 23 us
  Pallas kernels  23 us (99%)
    pallas_call x1, Pallas kernels, shards(): pl.pallas_call(functools.partial(kernel, size_x, size_y), out_shape=jax.S...  21.2 us
    pallas_call x1, Pallas kernels, shards(): pl.pallas_call(hand_over, out_shape=jax.ShapeDtypeStruct(out.shape, out.d...  1.82 us

profile of v8, /device:TPU:0, one launch (start us, length us, event | category | flops | bytes accessed | tf_op | source)
XLA Modules:
  0.0 23.0 jit_solution(1439025187840707954)
XLA Ops:
  0.0 21.2 %brick_encoder.1.source = bf16[32,4,4,512]{3,2,1,0:T(4,128)(2,1)} custom-call(s32[8,27]{1,0:T(8,128)} %ids_hbm.1, s32[1,8]{1,0:T(1,128)} %bitcast.4, bf16[512,512]{1,0:T(8,128)(2,1)} %bitcast.3, bf16[27,64,64]{2,1,0:T(8,128)(2,1)} %conv_hbm.1, f32[1,64]{1,0:T(1,128)} %bitcast.5, bf16[8,64,128]{2,1,0:T(8,128)(2,1)} %down_hbm.1), custom_call_target="tpu_custom_call" | custom-call | tf_op jit(solution)/shard_map/brick_encoder/pallas_call | solution.py:489
  21.2 1.8 %hand_over.1 = bf16[32,4,4,512]{3,2,1,0:T(4,128)(2,1)} custom-call(bf16[32,4,4,512]{3,2,1,0:T(4,128)(2,1)} %brick_encoder.1.source), custom_call_target="tpu_custom_call" | custom-call | tf_op jit(solution)/shard_map/hand_over/pallas_call | solution.py:541
